TPU v7x, 128 devices: a whole 4x4x4 slice. The times are simulated.
128 devices in a mesh: sec: 16 (over z, x), az: 8 (over y, core).
Axes of the slice: x: 4, y: 4, z: 4, core: 2. Of those that a mesh axis runs over, the one named last changes fastest.
Arguments:
- currents: float32 [256, 16, 1024], P(('sec', 'az')), may hold values from -6 to 6
- right_side: float32 [256, 16, 1024], P(('sec', 'az')), may hold values from -6 to 6
- counts: int32 [256], P(('sec', 'az')), may hold values from 128 to 1024, as said below
- inverse_blocks: bfloat16 [256, 1024, 1024], P(('sec', 'az')), may hold values from -0.1875 to 0.1875
- near_out: bfloat16 [256, 4, 128, 1024], P(('sec', 'az')), may hold values from -0.1875 to 0.1875
- near_in: bfloat16 [256, 4, 128, 1024], P(('sec', 'az')), may hold values from -0.5 to 0.5
- far_source_basis: bfloat16 [256, 32, 1024], P(('sec', 'az')), may hold values from -0.1875 to 0.1875
- far_target_basis: bfloat16 [256, 32, 1024], P(('sec', 'az')), may hold values from -1 to 1
- far_cores: bfloat16 [196608, 1024], P(('sec', 'az')), may hold values from -0.0390625 to 0.0390625
- far_target_device: int32 [196608, 1], P(('sec', 'az')), may hold values from 0 to 127; in each aligned block of 1536 rows (0 to 1535, 1536 to 3071, ...) at most 24 rows name the same one
- far_target_half: int32 [196608], P(('sec', 'az')), may hold values from 0 to 1
- far_source_half: int32 [196608], P(('sec', 'az')), may hold values from 0 to 1
Outputs:
- updated: float32 [256, 16, 1024], P(('sec', 'az'))
Inputs may be any that keep to these rules, and one draw needn't show every extreme that they name: `far_target_device`: in the rows of one device's far couplings no device is named more than 24 times, and some device exactly 24 times. `counts`: A multiple of 128; some subdomain has exactly 1024.
All inputs are finite; a program needn't handle non-finite values.
Results may differ from a plain program's by a relative error of at most 0.005.
Values may be sent and summed in bfloat16 or wider, within the bound.
No kernel may reach another device: no remote copies, remote signals or barrier semaphores. Data moves between devices by JAX's collectives and lax.ppermute only.
A program may use at most 64 MiB of HBM per device.

v0:
```python
import jax
import jax.numpy as jnp
from jax import lax
from jax.sharding import PartitionSpec as P


def passed_along(value, axis, steps):
    count = lax.axis_size(axis)
    initial, last = (max(0, -steps), min(count, count - steps))
    return lax.ppermute(value, axis, [(source, source + steps) for source in range(initial, last)])


def passed_along_2(block, axis, distance):
    devices = range(lax.axis_size(axis))
    route = [((i - distance) % len(devices), i) for i in devices]
    return lax.ppermute(block, axis, route)


def local(
    currents,
    right_side,
    counts,
    inverse_blocks,
    near_out,
    near_in,
    far_source_basis,
    far_target_basis,
    far_cores,
    far_target_device,
    far_target_half,
    far_source_half,
):
    sub_count, rhs_count, row_count = currents.shape
    far_rank = far_source_basis.shape[1]
    far_len = far_cores.shape[0]
    width = rhs_count * far_rank
    sec_count = lax.axis_size("sec")
    az_count = lax.axis_size("az")
    devices = sec_count * az_count
    capacity = 2 * far_len // devices
    row_mask = jnp.arange(row_count)[None, None, :] < counts[:, None, None]
    masked = jnp.where(row_mask, currents, 0.0).astype(jnp.bfloat16)
    coeffs = jnp.einsum(
        "srm,sdkm->sdrk", masked, near_out, preferred_element_type=jnp.float32
    ).astype(jnp.bfloat16)
    from_above = passed_along(coeffs[1, 0], "sec", 1)
    from_below = passed_along(coeffs[0, 1], "sec", -1)
    from_west = passed_along_2(coeffs[:, 2], "az", 1)
    from_east = passed_along_2(coeffs[:, 3], "az", -1)
    projected = jnp.einsum(
        "srm,skm->srk", masked, far_source_basis, preferred_element_type=jnp.float32
    ).astype(jnp.bfloat16)
    identity = jnp.eye(far_rank, dtype=jnp.bfloat16)
    spread = projected.transpose(0, 2, 1)[:, None, :, :, None] * identity[None, :, None, None, :]
    spread = spread.transpose(1, 2, 0, 3, 4).reshape(far_rank * far_rank, 2 * width)
    both_terms = jnp.dot(far_cores, spread, preferred_element_type=jnp.float32)
    flat_terms = jnp.where(
        far_source_half[:, None] == 0, both_terms[:, :width], both_terms[:, width:]
    ).astype(jnp.bfloat16)
    destination = far_target_device[:, 0]
    onehot = (destination[:, None] == jnp.arange(devices)[None, :]).astype(jnp.int32)
    slot_index = jnp.sum((jnp.cumsum(onehot, axis=0) - 1) * onehot, axis=1)
    position = destination * capacity + slot_index
    packed = jnp.zeros((devices * capacity, width), jnp.bfloat16).at[position].set(flat_terms)
    labels = jnp.full((devices * capacity,), -1, jnp.int32).at[position].set(far_target_half)
    received, recv_labels = (
        lax.all_to_all(
            packed.reshape(devices, capacity, width),
            ("sec", "az"),
            split_axis=0,
            concat_axis=0,
            tiled=True,
        ),
        lax.all_to_all(
            labels.reshape(devices, capacity),
            ("sec", "az"),
            split_axis=0,
            concat_axis=0,
            tiled=True,
        ),
    )
    received = received.reshape(devices * capacity, width)
    recv_labels = recv_labels.reshape(devices * capacity)
    selector = (recv_labels[None, :] == jnp.arange(sub_count)[:, None]).astype(jnp.bfloat16)
    far_sum = jnp.dot(selector, received, preferred_element_type=jnp.float32)
    far_in = far_sum.reshape(sub_count, rhs_count, far_rank).astype(jnp.bfloat16)
    from_minus = jnp.stack([from_above, coeffs[0, 0]])
    from_plus = jnp.stack([coeffs[1, 1], from_below])
    incoming = jnp.stack([from_minus, from_plus, from_west, from_east], axis=1)
    near_term = jnp.einsum("sdrk,sdkm->srm", incoming, near_in, preferred_element_type=jnp.float32)
    far_term = jnp.einsum(
        "srk,skm->srm", far_in, far_target_basis, preferred_element_type=jnp.float32
    )
    residual = (jnp.where(row_mask, right_side, 0.0) - near_term - far_term).astype(jnp.bfloat16)
    updated = jnp.einsum(
        "srn,smn->srm", residual, inverse_blocks, preferred_element_type=jnp.float32
    )
    return jnp.where(row_mask, updated, 0.0)


def solution(mesh):
    in_specs = (
        P(("sec", "az"), None, None),
        P(("sec", "az"), None, None),
        P(("sec", "az")),
        P(("sec", "az"), None, None),
        P(("sec", "az"), None, None, None),
        P(("sec", "az"), None, None, None),
        P(("sec", "az"), None, None),
        P(("sec", "az"), None, None),
        P(("sec", "az"), None),
        P(("sec", "az"), None),
        P(("sec", "az")),
        P(("sec", "az")),
    )
    out_specs = P(("sec", "az"), None, None)
    return jax.shard_map(local, mesh=mesh, in_specs=in_specs, out_specs=out_specs, check_vma=False)
```

profile of v0, /device:TPU:1, one launch (start us, length us, event | category | flops | bytes accessed | tf_op | source)
XLA Modules:
  0.0 123.7 jit_solution(11780850846503738172)
XLA Ops:
  0.0 0.0 copy-start
  0.0 0.0 copy-start.6
  0.0 0.0 copy-start.8
  0.0 0.0 copy-start.2
  0.0 0.0 copy-start.4
  0.0 0.9 reduce
  0.9 0.1 copy.32
  1.0 0.3 fusion.14
  1.4 0.0 copy-start.1
  1.4 1.0 copy-done.1
  2.4 1.3 %add_add_fusion = s32[128,12,128]{0,1,2:T(8,128)S(1)} fusion(s32[128,12,128]{0,1,2:T(8,128)} %copy-done.1, s32[128,12]{0,1:T(8,128)S(1)} %bitcast.68), kind=kLoop, calls=%fused_computation.20 | loop fusion | flops 393216 | bytes 1579008 | tf_op jit(solution)/shard_map/sub | solution.py:62
  3.7 0.3 copy.33
  3.9 0.5 fusion.16
  4.4 0.0 copy-done.6
  4.5 6.4 %scatter_custom_fusion = s32[3072]{0:T(1024)S(1)} fusion(s32[1536]{0:T(1024)S(1)} %fusion.33, s32[1536]{0:T(1024)} %param.22, s32[]{:T(128)} %constant.7.clone.1), kind=kCustom, calls=%fused_computation.52 | custom fusion | bytes 12800 | tf_op jit(solution)/shard_map/scatter | solution.py:65
  10.8 0.7 all_to_all.9
  11.6 11.5 %all-to-all-start = ((s32[128,1,24]{2,1,0:T(1,128)}), s32[128,1,24]{2,1,0:T(1,128)S(1)}, u32[]{:S(2)}, u32[]{:S(2)}) async-start(s32[128,1,24]{2,1,0:T(1,128)} %bitcast.19), calls=%async_computation | async-start | bytes 131072 | tf_op jit(solution)/shard_map/all_to_all | solution.py:74
  23.1 0.0 copy-done.8
  23.1 0.1 iota_compare_fusion.4
  23.2 0.0 copy-done.2
  23.2 0.0 copy-done.4
  23.2 0.1 fusion.13
  23.3 0.1 copy.35
  23.4 4.0 %broadcast_multiply_fusion = bf16[32,32,2,16,32]{4,3,2,1,0:T(8,128)(2,1)} fusion(bf16[32,32]{1,0:T(8,128)(2,1)S(1)} %fusion.29, bf16[32,2,16]{2,1,0:T(2,128)(2,1)S(1)} %copy.35), kind=kLoop, calls=%fused_computation.3 | loop fusion | flops 1048576 | bytes 2101248 | tf_op jit(solution)/shard_map/mul | solution.py:54
  27.4 0.0 copy-start.7
  27.4 12.4 %mul.34 = bf16[1024,1024]{1,0:T(8,128)(2,1)} reshape(bf16[32,32,2,16,32]{4,3,2,1,0:T(8,128)(2,1)} %broadcast_multiply_fusion) | data formatting | bytes 4194304 | tf_op jit(solution)/shard_map/mul | solution.py:54
  39.8 0.0 copy-done.7
  39.8 0.0 copy-done
  39.8 5.3 %convolution_bitcast_fusion = bf16[1536,1024]{0,1:T(8,128)(2,1)S(1)} fusion(bf16[1024,1024]{1,0:T(8,128)(2,1)} %mul.34, bf16[1536,1024]{1,0:T(8,128)(2,1)S(1)} %copy-done), kind=kOutput, calls=%fused_computation.2 | convolution fusion | flops 3221225472 | bytes 8388608 | tf_op jit(solution)/shard_map/dot_general | solution.py:56
  45.2 1.3 %fusion = bf16[1536,512]{0,1:T(8,128)(2,1)} fusion(bf16[1536,1024]{0,1:T(8,128)(2,1)S(1)} %convolution_bitcast_fusion, pred[1536]{0:T(1024)(128)(4,1)S(1)} %broadcast_compare_fusion), kind=kLoop, calls=%fused_computation.5 | loop fusion | flops 786432 | bytes 4720128 | tf_op jit(solution)/shard_map/convert_element_type | solution.py:59
  46.5 2.6 %copy.36 = bf16[1536,512]{1,0:T(8,128)(2,1)} copy(bf16[1536,512]{0,1:T(8,128)(2,1)} %fusion) | data formatting | bytes 3145728 | tf_op jit(solution)/shard_map/convert_element_type | solution.py:59
  49.1 9.9 %scatter_custom_fusion.1 = bf16[3072,512]{1,0:T(8,128)(2,1)} fusion(s32[1536]{0:T(1024)S(1)} %fusion.33, bf16[1536,512]{1,0:T(8,128)(2,1)} %copy.36, bf16[]{:T(256)} %constant.5.clone.1), kind=kCustom, calls=%fused_computation.8 | custom fusion | bytes 3146240 | tf_op jit(solution)/shard_map/scatter | solution.py:64
  59.0 0.0 all-to-all-done
  59.0 0.0 copy-start.3
  59.0 10.2 %all-to-all-start.1 = ((bf16[128,24,512]{2,1,0:T(8,128)(2,1)}), bf16[128,24,512]{2,1,0:T(8,128)(2,1)}, u32[]{:S(2)}, u32[]{:S(2)}) async-start(bf16[128,24,512]{2,1,0:T(8,128)(2,1)} %bitcast.65), calls=%async_computation.1 | async-start | bytes 6291456 | tf_op jit(solution)/shard_map/all_to_all | solution.py:67
  69.2 2.2 %fusion.12 = bf16[2,4,16,128]{3,2,1,0:T(8,128)(2,1)S(1)} fusion(bf16[2,4,128,1024]{3,2,1,0:T(8,128)(2,1)} %param.16, f32[2,16,1024]{2,1,0:T(8,128)S(1)} %copy-done.2, pred[2,1024]{1,0:T(4,128)(4,1)S(1)} %iota_compare_fusion.4), kind=kOutput, calls=%fused_computation.16 | convolution fusion | flops 33603584 | bytes 2263040 | tf_op jit(solution)/shard_map/srm,sdkm->sdrk/dot_general | solution.py:43
  71.4 3.3 %collective-permute-start = (bf16[16,128]{1,0:T(8,128)(2,1)S(1)}, bf16[16,128]{1,0:T(8,128)(2,1)S(1)}, u32[]{:S(2)}, u32[]{:S(2)}) collective-permute-start(bf16[16,128]{1,0:T(8,128)(2,1)S(1)} %get-tuple-element.5), channel_id=1, source_target_pairs={{0,8},{8,16},{16,24},{24,32},{32,40},{40,48},{48,56},{56,64},{64,7... | collective-permute-start | bytes 12296 | tf_op jit(solution)/shard_map/ppermute | solution.py:10
  74.7 1.3 %collective-permute-start.1 = (bf16[16,128]{1,0:T(8,128)(2,1)S(1)}, bf16[16,128]{1,0:T(8,128)(2,1)S(1)}, u32[]{:S(2)}, u32[]{:S(2)}) collective-permute-start(bf16[16,128]{1,0:T(8,128)(2,1)S(1)} %get-tuple-element.6), channel_id=1, source_target_pairs={{8,0},{16,8},{24,16},{32,24},{40,32},{48,40},{56,48},{64,56},{72,6... | collective-permute-start | bytes 12296 | tf_op jit(solution)/shard_map/ppermute | solution.py:10
  76.1 1.7 %collective-permute-start.2 = (bf16[2,16,128]{2,1,0:T(8,128)(2,1)S(1)}, bf16[2,16,128]{2,1,0:T(8,128)(2,1)S(1)}, u32[]{:S(2)}, u32[]{:S(2)}) collective-permute-start(bf16[2,16,128]{2,1,0:T(8,128)(2,1)S(1)} %get-tuple-element.9), channel_id=1, source_target_pairs={{7,0},{0,1},{1,2},{2,3},{3,4},{4,5},{5,6},{6,7},{15,8},{8,9},{9,10... | collective-permute-start | bytes 24584 | tf_op jit(solution)/shard_map/ppermute | solution.py:16
  77.8 0.0 collective-permute-start.3
  77.8 23.5 %collective-permute-done = bf16[16,128]{1,0:T(8,128)(2,1)S(1)} collective-permute-done((bf16[16,128]{1,0:T(8,128)(2,1)S(1)}, bf16[16,128]{1,0:T(8,128)(2,1)S(1)}, u32[]{:S(2)}, u32[]{:S(2)}) %collective-permute-start) | collective-permute-done | bytes 4128 | tf_op jit(solution)/shard_map/ppermute | solution.py:10
  101.3 2.9 %collective-permute-done.1 = bf16[16,128]{1,0:T(8,128)(2,1)S(1)} collective-permute-done((bf16[16,128]{1,0:T(8,128)(2,1)S(1)}, bf16[16,128]{1,0:T(8,128)(2,1)S(1)}, u32[]{:S(2)}, u32[]{:S(2)}) %collective-permute-start.1) | collective-permute-done | bytes 4128 | tf_op jit(solution)/shard_map/ppermute | solution.py:10
  104.2 0.0 collective-permute-done.2
  104.2 0.0 collective-permute-done.3
  104.2 0.0 copy-done.3
  104.2 2.0 %fusion.8 = f32[2,16,1024]{2,1,0:T(8,128)S(1)} fusion(bf16[2,4,128,1024]{3,2,1,0:T(8,128)(2,1)} %param.17, f32[2,16,1024]{2,1,0:T(8,128)S(1)} %copy-done.3, pred[2,1024]{1,0:T(4,128)(4,1)S(1)} %iota_compare_fusion.4, bf16[2,1,16,128]{3,2,0,1:T(8,128)(2,1)S(1)} %bitcast.70, bf16[2,1,16,128]{3,2,0,1:T(8,128)(2,1)S(1)} %bitcast.69, ...), kind=kOutput, calls=%fused_computation.13 | convolution fusion | flops 33669120 | bytes 2394112 | tf_op jit(solution)/shard_map/sdrk,sdkm->srm/dot_general | solution.py:90
  106.2 0.5 broadcast.65
  106.7 0.8 reduce.7
  107.5 0.1 eq.62
  107.6 3.2 %all-to-all-done.1 = bf16[128,24,512]{2,1,0:T(8,128)(2,1)} async-done(((bf16[128,24,512]{2,1,0:T(8,128)(2,1)}), bf16[128,24,512]{2,1,0:T(8,128)(2,1)}, u32[]{:S(2)}, u32[]{:S(2)}) %all-to-all-start.1) | async-done | bytes 3145760 | tf_op jit(solution)/shard_map/all_to_all | solution.py:67
  110.8 4.7 %copy.37 = bf16[512,3072]{1,0:T(8,128)(2,1)} copy(bf16[512,3072]{0,1:T(8,128)(2,1)} %bitcast.25) | data formatting | bytes 6291456 | tf_op jit(solution)/shard_map/dot_general | solution.py:85
  115.5 0.0 copy-start.5
  115.5 4.0 %convolution_convert_fusion.1 = bf16[2,16,32]{2,0,1:T(2,128)(2,1)S(1)} fusion(bf16[16,32,3072]{2,1,0:T(8,128)(2,1)} %bitcast.66, s32[3072]{0:T(1024)S(1)} %eq.62), kind=kOutput, calls=%fused_computation.17 | convolution fusion | flops 6298624 | bytes 3160064 | tf_op jit(solution)/shard_map/dot_general | solution.py:85
  119.6 0.0 copy-done.5
  119.6 4.1 %convolution_select_fusion = f32[2,16,1024]{2,1,0:T(8,128)} fusion(bf16[2,1024,1024]{2,1,0:T(8,128)(2,1)} %param.15, f32[2,16,1024]{2,1,0:T(8,128)S(1)} %fusion.8, bf16[2,32,1024]{2,1,0:T(8,128)(2,1)S(1)} %copy-done.5, pred[2,1024]{1,0:T(4,128)(4,1)S(1)} %iota_compare_fusion.4, bf16[2,16,32]{2,0,1:T(2,128)(2,1)S(1)} %convolution_convert_fusion.1), kind=kOutput, calls=%fused_computation.12 | convolution fusion | flops 69304320 | bytes 4591616 | tf_op jit(solution)/shard_map/srn,smn->srm/dot_general | solution.py:95
  (9 shorter events, 0.1 us)
Async XLA Ops:
  0.0 39.8 %copy-start = (bf16[1536,1024]{1,0:T(8,128)(2,1)S(1)}, bf16[1536,1024]{1,0:T(8,128)(2,1)}, u32[]{:S(2)}) copy-start(bf16[1536,1024]{1,0:T(8,128)(2,1)} %param.20) | copy-start | bytes 9437188
  0.0 4.4 %copy-start.6 = (s32[1536,1]{0,1:T(1,128)S(1)}, s32[1536,1]{0,1:T(1,128)}, u32[]{:S(2)}) copy-start(s32[1536,1]{0,1:T(1,128)} %param.21) | copy-start | bytes 18436
  0.0 23.1 %copy-start.8 = (s32[2]{0:T(128)S(1)}, s32[2]{0:T(128)}, u32[]{:S(2)}) copy-start(s32[2]{0:T(128)} %param.14) | copy-start | bytes 28
  0.0 23.2 %copy-start.2 = (f32[2,16,1024]{2,1,0:T(8,128)S(1)}, f32[2,16,1024]{2,1,0:T(8,128)}, u32[]{:S(2)}) copy-start(f32[2,16,1024]{2,1,0:T(8,128)} %param.12) | copy-start | bytes 393220
  0.0 23.2 %copy-start.4 = (bf16[2,32,1024]{2,1,0:T(8,128)(2,1)S(1)}, bf16[2,32,1024]{2,1,0:T(8,128)(2,1)}, u32[]{:S(2)}) copy-start(bf16[2,32,1024]{2,1,0:T(8,128)(2,1)} %param.18) | copy-start | bytes 393220
  1.4 1.0 copy-start.1
  11.6 47.5 %all-to-all-start = ((s32[128,1,24]{2,1,0:T(1,128)}), s32[128,1,24]{2,1,0:T(1,128)S(1)}, u32[]{:S(2)}, u32[]{:S(2)}) async-start(s32[128,1,24]{2,1,0:T(1,128)} %bitcast.19), calls=%async_computation | async-start | bytes 131072 | tf_op jit(solution)/shard_map/all_to_all | solution.py:74
  27.4 12.4 %copy-start.7 = (s32[1536]{0:T(1024)S(1)}, s32[1536]{0:T(1024)}, u32[]{:S(2)}) copy-start(s32[1536]{0:T(1024)} %param.23) | copy-start | bytes 18436
  59.0 45.2 %copy-start.3 = (f32[2,16,1024]{2,1,0:T(8,128)S(1)}, f32[2,16,1024]{2,1,0:T(8,128)}, u32[]{:S(2)}) copy-start(f32[2,16,1024]{2,1,0:T(8,128)} %param.13) | copy-start | bytes 393220
  59.0 51.8 %all-to-all-start.1 = ((bf16[128,24,512]{2,1,0:T(8,128)(2,1)}), bf16[128,24,512]{2,1,0:T(8,128)(2,1)}, u32[]{:S(2)}, u32[]{:S(2)}) async-start(bf16[128,24,512]{2,1,0:T(8,128)(2,1)} %bitcast.65), calls=%async_computation.1 | async-start | bytes 6291456 | tf_op jit(solution)/shard_map/all_to_all | solution.py:67
  71.4 29.8 %collective-permute-start = (bf16[16,128]{1,0:T(8,128)(2,1)S(1)}, bf16[16,128]{1,0:T(8,128)(2,1)S(1)}, u32[]{:S(2)}, u32[]{:S(2)}) collective-permute-start(bf16[16,128]{1,0:T(8,128)(2,1)S(1)} %get-tuple-element.5), channel_id=1, source_target_pairs={{0,8},{8,16},{16,24},{24,32},{32,40},{40,48},{48,56},{56,64},{64,7... | collective-permute-start | bytes 12296 | tf_op jit(solution)/shard_map/ppermute | solution.py:10
  74.7 29.4 %collective-permute-start.1 = (bf16[16,128]{1,0:T(8,128)(2,1)S(1)}, bf16[16,128]{1,0:T(8,128)(2,1)S(1)}, u32[]{:S(2)}, u32[]{:S(2)}) collective-permute-start(bf16[16,128]{1,0:T(8,128)(2,1)S(1)} %get-tuple-element.6), channel_id=1, source_target_pairs={{8,0},{16,8},{24,16},{32,24},{40,32},{48,40},{56,48},{64,56},{72,6... | collective-permute-start | bytes 12296 | tf_op jit(solution)/shard_map/ppermute | solution.py:10
  76.1 28.1 %collective-permute-start.2 = (bf16[2,16,128]{2,1,0:T(8,128)(2,1)S(1)}, bf16[2,16,128]{2,1,0:T(8,128)(2,1)S(1)}, u32[]{:S(2)}, u32[]{:S(2)}) collective-permute-start(bf16[2,16,128]{2,1,0:T(8,128)(2,1)S(1)} %get-tuple-element.9), channel_id=1, source_target_pairs={{7,0},{0,1},{1,2},{2,3},{3,4},{4,5},{5,6},{6,7},{15,8},{8,9},{9,10... | collective-permute-start | bytes 24584 | tf_op jit(solution)/shard_map/ppermute | solution.py:16
  77.8 26.4 %collective-permute-start.3 = (bf16[2,16,128]{2,1,0:T(8,128)(2,1)S(1)}, bf16[2,16,128]{2,1,0:T(8,128)(2,1)S(1)}, u32[]{:S(2)}, u32[]{:S(2)}) collective-permute-start(bf16[2,16,128]{2,1,0:T(8,128)(2,1)S(1)} %get-tuple-element.10), channel_id=1, source_target_pairs={{1,0},{2,1},{3,2},{4,3},{5,4},{6,5},{7,6},{0,7},{9,8},{10,9},{11,1... | collective-permute-start | bytes 24584 | tf_op jit(solution)/shard_map/ppermute | solution.py:16
  115.5 4.1 %copy-start.5 = (bf16[2,32,1024]{2,1,0:T(8,128)(2,1)S(1)}, bf16[2,32,1024]{2,1,0:T(8,128)(2,1)}, u32[]{:S(2)}) copy-start(bf16[2,32,1024]{2,1,0:T(8,128)(2,1)} %param.19) | copy-start | bytes 393220
where the time goes:
time: 125 us; the launch traced here: 124 us
  local copies, waits for them, and re-layouts  38.8 us (31%)
  waiting for transfers between devices  29.6 us (24%)
  starting transfers between devices  28 us (22%)
  matrix products  17.9 us (14%)
  other arithmetic  9.22 us (7%)
    ppermute x2, waiting for transfers between devices, passed_along(): lax.ppermute(value, axis, [(source, source + steps) for source in range(i...  26.4 us
    mul x1, local copies, waits for them, and re-layouts, local(): projected.transpose(0, 2, 1)[:, None, :, :, None]  12.4 us
    all_to_all x1, starting transfers between devices, local(): lax.all_to_all(labels.reshape(devices, capacity), ('sec', 'az'), split_ax...  11.5 us
    all_to_all x1, starting transfers between devices, local(): lax.all_to_all(packed.reshape(devices, capacity, width), ('sec', 'az'), s...  10.2 us
    scatter x1, local copies, waits for them, and re-layouts, local(): jnp.zeros((devices * capacity, width), jnp.bfloat16).at[position]  9.94 us
    scatter x1, local copies, waits for them, and re-layouts, local(): jnp.full((devices * capacity,), -1, jnp.int32).at[position]  6.36 us
    dot_general x1, matrix products, local(): both_terms = jnp.dot(far_cores, spread, preferred_element_type=jnp.float32)  5.33 us
    dot_general x1, local copies, waits for them, and re-layouts, local(): far_sum = jnp.dot(selector, received, preferred_element_type=jnp.float32)  4.69 us
  transfers between devices with their start and end apart: 6, of which 3 were waited for; matrix products, arithmetic and copies ran while one was open for 34% of the time, Pallas kernels for 0%

commit v1 on v0

v1 whole, which is shorter than its diff:
```python
import jax
import jax.numpy as jnp
from jax import lax
from jax.experimental import pallas as pl
from jax.experimental.pallas import tpu as pltpu
from jax.sharding import PartitionSpec as P

BF = jnp.bfloat16
F32 = jnp.float32
VMEM = pl.BlockSpec(memory_space=pltpu.VMEM)
SMEM = pl.BlockSpec(memory_space=pltpu.SMEM)
ANY = pl.BlockSpec(memory_space=pl.ANY)
MIB = 1024 * 1024
NT = (((1,), (1,)), ((), ()))


def iota(shape, dim):
    return lax.broadcasted_iota(jnp.int32, shape, dim)


def dot(a, b, dims=(((1,), (0,)), ((), ()))):
    return lax.dot_general(a, b, dims, preferred_element_type=F32)


def keep_rows(counts, values, sub):
    return jnp.where(iota(values.shape, 1) < counts[sub], values, 0.0)


def far_out_kernel(counts, currents, basis, device, target_half, source_half, cores_hbm, out, cores, staged, sems):
    chunks, _, width = cores.shape
    rhs_count = currents.shape[1]
    rank = basis.shape[1]
    targets = staged.shape[0] // chunks
    copies = [
        pltpu.make_async_copy(cores_hbm.at[:, pl.ds(k * width, width)], cores.at[k], sems.at[k]) for k in range(chunks)
    ]
    for copy in copies:
        copy.start()
    place = source_half[...] * targets + device[...] * 2 + target_half[...]
    place = place.reshape(1, place.shape[-1])
    onehot = (iota((2 * targets, place.shape[1]), 0) == place).astype(BF)
    lanes = staged.shape[1]
    repeat = (iota((rhs_count, lanes), 1) % rhs_count == iota((rhs_count, lanes), 0)).astype(BF)
    diagonal = iota((width, lanes), 0) // rank == iota((width, lanes), 1) // rhs_count
    spread = []
    for sub in range(2):
        masked = keep_rows(counts, currents[sub], sub).astype(BF)
        projected = dot(basis[sub], masked, NT).astype(BF)
        tiled = jnp.concatenate([dot(projected, repeat)] * (width // rank), axis=0)
        spread.append(jnp.where(diagonal, tiled, 0.0).astype(BF))
    for k in range(chunks):
        copies[k].wait()
        sums = dot(onehot, cores[k]).astype(BF)
        terms = dot(sums[:targets], spread[0]) + dot(sums[targets:], spread[1])
        staged[pl.ds(k, targets, stride=chunks), :] = terms
    out[...] = staged[...].reshape(out.shape).astype(BF)


def near_out_kernel(counts, currents, near_out, up, down, west, east, kept):
    rank = up.shape[1]
    for sub in range(2):
        masked = keep_rows(counts, currents[sub], sub).astype(BF)
        factors = near_out[sub].reshape(4 * rank, near_out.shape[3])
        coeffs = dot(masked, factors, NT).astype(BF)
        west[sub] = coeffs[:, 2 * rank : 3 * rank]
        east[sub] = coeffs[:, 3 * rank :]
        if sub == 0:
            kept[0] = coeffs[:, :rank]
            down[...] = coeffs[:, rank : 2 * rank]
        else:
            up[...] = coeffs[:, :rank]
            kept[1] = coeffs[:, rank : 2 * rank]


def solve_kernel(counts, right_side, above, below, west, east, kept, near_in, basis, inverse, base, weights):
    rank = above.shape[1]
    rhs_count = right_side.shape[1]
    for sub in range(2):
        if sub == 0:
            incoming = [above[...], kept[1], west[0], east[0]]
        else:
            incoming = [kept[0], below[...], west[1], east[1]]
        near_term = dot(jnp.concatenate(incoming, axis=1), near_in[sub].reshape(4 * rank, near_in.shape[3]))
        rest = keep_rows(counts, right_side[sub], sub) - near_term
        high = rest.astype(BF)
        low = (rest - high.astype(F32)).astype(BF)
        solved = dot(jnp.concatenate([high, low, basis[sub]], axis=0), inverse[sub], NT)
        base[sub] = solved[:rhs_count] + solved[rhs_count : 2 * rhs_count]
        weights[sub] = solved[2 * rhs_count :].astype(BF)


def far_in_kernel(counts, received, base, weights, out):
    rhs_count = base.shape[1]
    rank = weights.shape[1]
    sums = jnp.sum(received[...].astype(F32), axis=0)
    chunks = sums.shape[0] // 2
    lanes = sums.shape[1]
    own = iota((rhs_count, lanes), 1) % rhs_count == iota((rhs_count, lanes), 0)
    select = (iota((chunks * lanes, rank), 0) // rhs_count == iota((chunks * lanes, rank), 1)).astype(BF)
    for sub in range(2):
        pieces = [jnp.where(own, sums[sub * chunks + k : sub * chunks + k + 1], 0.0) for k in range(chunks)]
        far_in = dot(jnp.concatenate(pieces, axis=1).astype(BF), select).astype(BF)
        out[sub] = keep_rows(counts, base[sub] - dot(far_in, weights[sub]), sub)


def call(kernel, out_shape, in_specs, flops, moved, scratch=()):
    return pl.pallas_call(
        kernel,
        out_shape=out_shape,
        in_specs=in_specs,
        out_specs=jax.tree.map(lambda _: VMEM, out_shape),
        scratch_shapes=scratch,
        compiler_params=pltpu.CompilerParams(vmem_limit_bytes=40 * MIB),
        cost_estimate=pl.CostEstimate(flops=flops, bytes_accessed=moved, transcendentals=0),
    )


def shape(dims, dtype=BF):
    return jax.ShapeDtypeStruct(dims, dtype)


def local(
    currents,
    right_side,
    counts,
    inverse_blocks,
    near_out,
    near_in,
    far_source_basis,
    far_target_basis,
    far_cores,
    far_target_device,
    far_target_half,
    far_source_half,
):
    _, rhs_count, row_count = currents.shape
    far_rank = far_source_basis.shape[1]
    near_rank = near_out.shape[2]
    far_len = far_cores.shape[0]
    sec_count = lax.axis_size("sec")
    az_count = lax.axis_size("az")
    devices = sec_count * az_count
    width = 256
    chunks = far_cores.shape[1] // width
    lanes = width // far_rank * rhs_count

    packed = call(
        far_out_kernel,
        shape((devices, 2 * chunks, lanes)),
        [SMEM, VMEM, VMEM, VMEM, VMEM, VMEM, ANY],
        2 * 4 * devices * far_len * row_count,
        far_cores.size * 2,
        [
            pltpu.VMEM((chunks, far_len, width), BF),
            pltpu.VMEM((2 * devices * chunks, lanes), F32),
            pltpu.SemaphoreType.DMA((chunks,)),
        ],
    )(
        counts,
        currents,
        far_source_basis,
        far_target_device.reshape(1, far_len),
        far_target_half.reshape(1, far_len),
        far_source_half.reshape(1, far_len),
        far_cores,
    )
    received = lax.all_to_all(packed, ("sec", "az"), split_axis=0, concat_axis=0, tiled=True)

    piece = shape((rhs_count, near_rank))
    pair = shape((2, rhs_count, near_rank))
    up, down, west, east, kept = call(
        near_out_kernel,
        (piece, piece, pair, pair, pair),
        [SMEM, VMEM, VMEM],
        2 * near_out.size * rhs_count,
        near_out.size * 2,
    )(counts, currents, near_out)
    above = lax.ppermute(up, "sec", [(s, s + 1) for s in range(sec_count - 1)])
    below = lax.ppermute(down, "sec", [(s + 1, s) for s in range(sec_count - 1)])
    from_west = lax.ppermute(west, "az", [(a, (a + 1) % az_count) for a in range(az_count)])
    from_east = lax.ppermute(east, "az", [((a + 1) % az_count, a) for a in range(az_count)])

    base, weights = call(
        solve_kernel,
        (shape((2, rhs_count, row_count), F32), shape((2, far_rank, row_count))),
        [SMEM] + [VMEM] * 9,
        2 * 2 * inverse_blocks.size * rhs_count,
        inverse_blocks.size * 2 + near_in.size * 2,
    )(counts, right_side, above, below, from_west, from_east, kept, near_in, far_target_basis, inverse_blocks)

    return call(
        far_in_kernel,
        shape((2, rhs_count, row_count), F32),
        [SMEM] + [VMEM] * 3,
        2 * 2 * rhs_count * far_rank * row_count,
        received.size * 2,
    )(counts, received, base, weights)


def solution(mesh):
    in_specs = (
        P(("sec", "az"), None, None),
        P(("sec", "az"), None, None),
        P(("sec", "az")),
        P(("sec", "az"), None, None),
        P(("sec", "az"), None, None, None),
        P(("sec", "az"), None, None, None),
        P(("sec", "az"), None, None),
        P(("sec", "az"), None, None),
        P(("sec", "az"), None),
        P(("sec", "az"), None),
        P(("sec", "az")),
        P(("sec", "az")),
    )
    out_specs = P(("sec", "az"), None, None)
    return jax.shard_map(local, mesh=mesh, in_specs=in_specs, out_specs=out_specs, check_vma=False)
```

time: 125 us -> 45.9 us (0.37)
  the two profiles are of different devices: /device:TPU:1 before, /device:TPU:6 now
where the time goes in v1:
time: 45.9 us; the launch traced here: 45.4 us
  starting transfers between devices  19.3 us (42%)
  Pallas kernels  12.1 us (26%)
  local copies, waits for them, and re-layouts  8.65 us (19%)
  waiting for transfers between devices  5.25 us (11%)
    all_to_all x1, starting transfers between devices, local(): lax.all_to_all(packed, ('sec', 'az'), split_axis=0, concat_axis=0, tiled=...  10.5 us
    unnamed x24, local copies, waits for them, and re-layouts  7.25 us
    pallas_call x1, Pallas kernels, local(): call(far_out_kernel, shape((devices, 2 * chunks, lanes)), [SMEM, VMEM, VM...  7.02 us
    ppermute x1, waiting for transfers between devices, local(): lax.ppermute(down, 'sec', [(s + 1, s) for s in range(sec_count - 1)])  5.24 us
    ppermute x1, starting transfers between devices, local(): above = lax.ppermute(up, 'sec', [(s, s + 1) for s in range(sec_count - 1)])  3.48 us
    ppermute x1, starting transfers between devices, local(): lax.ppermute(east, 'az', [((a + 1) % az_count, a) for a in range(az_count)])  2.81 us
    ppermute x1, starting transfers between devices, local(): lax.ppermute(down, 'sec', [(s + 1, s) for s in range(sec_count - 1)])  2.35 us
    pallas_call x1, Pallas kernels, local(): call(solve_kernel, (shape((2, rhs_count, row_count), F32), shape((2, far_...  2.16 us
  transfers between devices with their start and end apart: 5, of which 1 were waited for; matrix products, arithmetic and copies ran while one was open for 0% of the time, Pallas kernels for 7%

profile of v1, /device:TPU:6, one launch (start us, length us, event | category | flops | bytes accessed | tf_op | source)
XLA Modules:
  0.0 45.4 jit_solution(2333730586097070388)
XLA Ops:
  0.0 0.7 %reshape.10.target_half = s32[1,1536]{1,0:T(1,128)S(1)} reshape(s32[1536]{0:T(1024)} %param.22) | data formatting | bytes 12288 | tf_op jit(solution)/shard_map/reshape | solution.py:163
  0.7 0.7 %reshape.11.source_half = s32[1,1536]{1,0:T(1,128)S(1)} reshape(s32[1536]{0:T(1024)} %param.23) | data formatting | bytes 12288 | tf_op jit(solution)/shard_map/reshape | solution.py:164
  1.4 0.0 copy-start.3
  1.4 0.9 %copy-done.3 = f32[2,16,1024]{2,1,0:T(8,128)S(1)} copy-done((f32[2,16,1024]{2,1,0:T(8,128)S(1)}, f32[2,16,1024]{2,1,0:T(8,128)}, u32[]{:S(2)}) %copy-start.3) | copy-done | bytes 131096
  2.3 0.0 copy-start.7
  2.3 0.7 %copy-done.7 = s32[2]{0:T(128)S(1)} copy-done((s32[2]{0:T(128)S(1)}, s32[2]{0:T(128)}, u32[]{:S(2)}) %copy-start.7) | copy-done | bytes 32
  3.0 0.0 copy-start.9
  3.0 1.9 %copy-done.9 = bf16[1536,1024]{1,0:T(8,128)(2,1)S(1)} copy-done((bf16[1536,1024]{1,0:T(8,128)(2,1)S(1)}, bf16[1536,1024]{1,0:T(8,128)(2,1)}, u32[]{:S(2)}) %copy-start.9) | copy-done | bytes 3145752
  4.9 0.0 copy-start.10
  4.9 0.9 %copy-done.10 = bf16[2,32,1024]{2,1,0:T(8,128)(2,1)S(1)} copy-done((bf16[2,32,1024]{2,1,0:T(8,128)(2,1)S(1)}, bf16[2,32,1024]{2,1,0:T(8,128)(2,1)}, u32[]{:S(2)}) %copy-start.10) | copy-done | bytes 131096
  5.8 0.0 copy-start.11
  5.8 0.7 %copy-done.11 = s32[1536,1]{0,1:T(1,128)S(1)} copy-done((s32[1536,1]{0,1:T(1,128)S(1)}, s32[1536,1]{0,1:T(1,128)}, u32[]{:S(2)}) %copy-start.11) | copy-done | bytes 6168
  6.5 0.0 copy-start.1
  6.5 0.0 copy-start.4
  6.5 0.0 copy-start.8
  6.5 0.0 copy-start.5
  6.5 0.0 copy-start.6
  6.5 7.0 %shard_map.118 = bf16[128,8,128]{2,1,0:T(8,128)(2,1)} custom-call(s32[2]{0:T(128)S(1)} %copy-done.7, f32[2,16,1024]{2,1,0:T(8,128)S(1)} %copy-done.3, bf16[2,32,1024]{2,1,0:T(8,128)(2,1)S(1)} %copy-done.10, s32[1,1536]{1,0:T(1,128)S(1)} %bitcast.1, s32[1,1536]{1,0:T(1,128)S(1)} %reshape.10.target_half, s32[1,1536]{1,0:T(1,128)S(1)} %reshape.11.source_half, ...), custom_call_target="tpu_custom_call" | custom-call | flops 1610612736 | bytes 3145728 | tf_op jit(solution)/shard_map/pallas_call | solution.py:147
  13.5 10.5 %all-to-all-start = ((bf16[128,8,128]{2,1,0:T(8,128)(2,1)}), bf16[128,8,128]{2,1,0:T(8,128)(2,1)S(1)}, u32[]{:S(2)}, u32[]{:S(2)}) async-start(bf16[128,8,128]{2,1,0:T(8,128)(2,1)} %shard_map.118), calls=%async_computation | async-start | bytes 524288 | tf_op jit(solution)/shard_map/all_to_all | solution.py:167
  24.0 0.0 copy-done.1
  24.0 0.0 copy-done.4
  24.0 0.0 copy-done.8
  24.0 0.0 copy-start.2
  24.0 1.2 %shard_map.119 = (bf16[16,128]{1,0:T(8,128)(2,1)S(1)}, bf16[16,128]{1,0:T(8,128)(2,1)S(1)}, bf16[2,16,128]{2,1,0:T(8,128)(2,1)S(1)}, bf16[2,16,128]{2,1,0:T(8,128)(2,1)S(1)}, bf16[2,16,128]{2,1,0:T(8,128)(2,1)S(1)}) custom-call(s32[2]{0:T(128)S(1)} %copy-done.8, f32[2,16,1024]{2,1,0:T(8,128)S(1)} %copy-done.4, bf16[2,4,128,1024]{3,2,1,0:T(8,128)(2,1)S(1)} %copy-done.1), custom_call_target="tpu_custom_call" | custom-call | flops 33554432 | bytes 2097152 | tf_op jit(solution)/shard_map/pallas_call | solution.py:171
  25.2 0.2 collective-permute-start.2
  25.4 2.8 %collective-permute-start.3 = (bf16[2,16,128]{2,1,0:T(8,128)(2,1)S(1)}, bf16[2,16,128]{2,1,0:T(8,128)(2,1)S(1)}, u32[]{:S(2)}, u32[]{:S(2)}) collective-permute-start(bf16[2,16,128]{2,1,0:T(8,128)(2,1)S(1)} %get-tuple-element.15), channel_id=1, source_target_pairs={{1,0},{2,1},{3,2},{4,3},{5,4},{6,5},{7,6},{0,7},{9,8},{10,9},{11,1... | collective-permute-start | bytes 24584 | tf_op jit(solution)/shard_map/ppermute | solution.py:181
  28.2 3.5 %collective-permute-start = (bf16[16,128]{1,0:T(8,128)(2,1)S(1)}, bf16[16,128]{1,0:T(8,128)(2,1)S(1)}, u32[]{:S(2)}, u32[]{:S(2)}) collective-permute-start(bf16[16,128]{1,0:T(8,128)(2,1)S(1)} %get-tuple-element.12), channel_id=1, source_target_pairs={{0,8},{8,16},{16,24},{24,32},{32,40},{40,48},{48,56},{56,64},{64,7... | collective-permute-start | bytes 12296 | tf_op jit(solution)/shard_map/ppermute | solution.py:178
  31.7 2.4 %collective-permute-start.1 = (bf16[16,128]{1,0:T(8,128)(2,1)S(1)}, bf16[16,128]{1,0:T(8,128)(2,1)S(1)}, u32[]{:S(2)}, u32[]{:S(2)}) collective-permute-start(bf16[16,128]{1,0:T(8,128)(2,1)S(1)} %get-tuple-element.13), channel_id=1, source_target_pairs={{8,0},{16,8},{24,16},{32,24},{40,32},{48,40},{56,48},{64,56},{72,6... | collective-permute-start | bytes 12296 | tf_op jit(solution)/shard_map/ppermute | solution.py:179
  34.0 0.0 collective-permute-done.above
  34.0 5.2 %collective-permute-done.1.below = bf16[16,128]{1,0:T(8,128)(2,1)S(1)} collective-permute-done((bf16[16,128]{1,0:T(8,128)(2,1)S(1)}, bf16[16,128]{1,0:T(8,128)(2,1)S(1)}, u32[]{:S(2)}, u32[]{:S(2)}) %collective-permute-start.1) | collective-permute-done | bytes 4128 | tf_op jit(solution)/shard_map/ppermute | solution.py:179
  39.3 0.0 collective-permute-done.2.west
  39.3 0.0 collective-permute-done.3.east
  39.3 0.0 copy-done.5
  39.3 0.0 copy-done.6
  39.3 0.0 copy-done.2
  39.3 0.0 copy-start
  39.3 2.2 %copy-done = bf16[2,1024,1024]{2,1,0:T(8,128)(2,1)S(1)} copy-done((bf16[2,1024,1024]{2,1,0:T(8,128)(2,1)S(1)}, bf16[2,1024,1024]{2,1,0:T(8,128)(2,1)}, u32[]{:S(2)}) %copy-start) | copy-done | bytes 4194328
  41.5 2.2 %shard_map.120 = (f32[2,16,1024]{2,1,0:T(8,128)S(1)}, bf16[2,32,1024]{2,1,0:T(8,128)(2,1)S(1)}) custom-call(s32[2]{0:T(128)S(1)} %copy-done.8, f32[2,16,1024]{2,1,0:T(8,128)S(1)} %copy-done.5, bf16[16,128]{1,0:T(8,128)(2,1)S(1)} %collective-permute-done.above, bf16[16,128]{1,0:T(8,128)(2,1)S(1)} %collective-permute-done.1.below, ...), custom_call_target="tpu_custom_call" | custom-call | flops 134217728 | bytes 6291456 | tf_op jit(solution)/shard_map/pallas_call | solution.py:183
  43.7 0.0 all-to-all-done.received
  43.7 1.8 %shard_map.121 = f32[2,16,1024]{2,1,0:T(8,128)} custom-call(s32[2]{0:T(128)S(1)} %copy-done.8, bf16[128,8,128]{2,1,0:T(8,128)(2,1)S(1)} %all-to-all-done.received, f32[2,16,1024]{2,1,0:T(8,128)S(1)} %get-tuple-element.17.base, bf16[2,32,1024]{2,1,0:T(8,128)(2,1)S(1)} %get-tuple-element.18.weights), custom_call_target="tpu_custom_call" | custom-call | flops 2097152 | bytes 262144 | tf_op jit(solution)/shard_map/pallas_call | solution.py:191
Async XLA Ops:
  1.4 0.9 %copy-start.3 = (f32[2,16,1024]{2,1,0:T(8,128)S(1)}, f32[2,16,1024]{2,1,0:T(8,128)}, u32[]{:S(2)}) copy-start(f32[2,16,1024]{2,1,0:T(8,128)} %currents.3) | copy-start | bytes 393220
  2.3 0.7 %copy-start.7 = (s32[2]{0:T(128)S(1)}, s32[2]{0:T(128)}, u32[]{:S(2)}) copy-start(s32[2]{0:T(128)} %counts.7) | copy-start | bytes 28
  3.0 1.9 %copy-start.9 = (bf16[1536,1024]{1,0:T(8,128)(2,1)S(1)}, bf16[1536,1024]{1,0:T(8,128)(2,1)}, u32[]{:S(2)}) copy-start(bf16[1536,1024]{1,0:T(8,128)(2,1)} %cores_hbm.1) | copy-start | bytes 9437188
  4.9 0.9 %copy-start.10 = (bf16[2,32,1024]{2,1,0:T(8,128)(2,1)S(1)}, bf16[2,32,1024]{2,1,0:T(8,128)(2,1)}, u32[]{:S(2)}) copy-start(bf16[2,32,1024]{2,1,0:T(8,128)(2,1)} %basis.2) | copy-start | bytes 393220
  5.8 0.7 %copy-start.11 = (s32[1536,1]{0,1:T(1,128)S(1)}, s32[1536,1]{0,1:T(1,128)}, u32[]{:S(2)}) copy-start(s32[1536,1]{0,1:T(1,128)} %param.21) | copy-start | bytes 18436
  6.5 17.5 %copy-start.1 = (bf16[2,4,128,1024]{3,2,1,0:T(8,128)(2,1)S(1)}, bf16[2,4,128,1024]{3,2,1,0:T(8,128)(2,1)}, u32[]{:S(2)}) copy-start(bf16[2,4,128,1024]{3,2,1,0:T(8,128)(2,1)} %near_out.1) | copy-start | bytes 6291460
  6.5 17.5 %copy-start.4 = (f32[2,16,1024]{2,1,0:T(8,128)S(1)}, f32[2,16,1024]{2,1,0:T(8,128)}, u32[]{:S(2)}) copy-start(f32[2,16,1024]{2,1,0:T(8,128)} %currents.3) | copy-start | bytes 393220
  6.5 17.6 %copy-start.8 = (s32[2]{0:T(128)S(1)}, s32[2]{0:T(128)}, u32[]{:S(2)}) copy-start(s32[2]{0:T(128)} %counts.7) | copy-start | bytes 28
  6.5 32.8 %copy-start.5 = (f32[2,16,1024]{2,1,0:T(8,128)S(1)}, f32[2,16,1024]{2,1,0:T(8,128)}, u32[]{:S(2)}) copy-start(f32[2,16,1024]{2,1,0:T(8,128)} %right_side.1) | copy-start | bytes 393220
  6.5 32.8 %copy-start.6 = (bf16[2,32,1024]{2,1,0:T(8,128)(2,1)S(1)}, bf16[2,32,1024]{2,1,0:T(8,128)(2,1)}, u32[]{:S(2)}) copy-start(bf16[2,32,1024]{2,1,0:T(8,128)(2,1)} %basis.3) | copy-start | bytes 393220
  13.5 30.2 %all-to-all-start = ((bf16[128,8,128]{2,1,0:T(8,128)(2,1)}), bf16[128,8,128]{2,1,0:T(8,128)(2,1)S(1)}, u32[]{:S(2)}, u32[]{:S(2)}) async-start(bf16[128,8,128]{2,1,0:T(8,128)(2,1)} %shard_map.118), calls=%async_computation | async-start | bytes 524288 | tf_op jit(solution)/shard_map/all_to_all | solution.py:167
  24.0 15.3 %copy-start.2 = (bf16[2,4,128,1024]{3,2,1,0:T(8,128)(2,1)S(1)}, bf16[2,4,128,1024]{3,2,1,0:T(8,128)(2,1)}, u32[]{:S(2)}) copy-start(bf16[2,4,128,1024]{3,2,1,0:T(8,128)(2,1)} %near_in.1) | copy-start | bytes 6291460
  25.2 14.1 %collective-permute-start.2 = (bf16[2,16,128]{2,1,0:T(8,128)(2,1)S(1)}, bf16[2,16,128]{2,1,0:T(8,128)(2,1)S(1)}, u32[]{:S(2)}, u32[]{:S(2)}) collective-permute-start(bf16[2,16,128]{2,1,0:T(8,128)(2,1)S(1)} %get-tuple-element.14), channel_id=1, source_target_pairs={{0,1},{1,2},{2,3},{3,4},{4,5},{5,6},{6,7},{7,0},{8,9},{9,10},{10,1... | collective-permute-start | bytes 24584 | tf_op jit(solution)/shard_map/ppermute | solution.py:180
  25.4 13.9 %collective-permute-start.3 = (bf16[2,16,128]{2,1,0:T(8,128)(2,1)S(1)}, bf16[2,16,128]{2,1,0:T(8,128)(2,1)S(1)}, u32[]{:S(2)}, u32[]{:S(2)}) collective-permute-start(bf16[2,16,128]{2,1,0:T(8,128)(2,1)S(1)} %get-tuple-element.15), channel_id=1, source_target_pairs={{1,0},{2,1},{3,2},{4,3},{5,4},{6,5},{7,6},{0,7},{9,8},{10,9},{11,1... | collective-permute-start | bytes 24584 | tf_op jit(solution)/shard_map/ppermute | solution.py:181
  28.2 5.8 %collective-permute-start = (bf16[16,128]{1,0:T(8,128)(2,1)S(1)}, bf16[16,128]{1,0:T(8,128)(2,1)S(1)}, u32[]{:S(2)}, u32[]{:S(2)}) collective-permute-start(bf16[16,128]{1,0:T(8,128)(2,1)S(1)} %get-tuple-element.12), channel_id=1, source_target_pairs={{0,8},{8,16},{16,24},{24,32},{32,40},{40,48},{48,56},{56,64},{64,7... | collective-permute-start | bytes 12296 | tf_op jit(solution)/shard_map/ppermute | solution.py:178
  31.7 7.6 %collective-permute-start.1 = (bf16[16,128]{1,0:T(8,128)(2,1)S(1)}, bf16[16,128]{1,0:T(8,128)(2,1)S(1)}, u32[]{:S(2)}, u32[]{:S(2)}) collective-permute-start(bf16[16,128]{1,0:T(8,128)(2,1)S(1)} %get-tuple-element.13), channel_id=1, source_target_pairs={{8,0},{16,8},{24,16},{32,24},{40,32},{48,40},{56,48},{64,56},{72,6... | collective-permute-start | bytes 12296 | tf_op jit(solution)/shard_map/ppermute | solution.py:179
  39.3 2.2 %copy-start = (bf16[2,1024,1024]{2,1,0:T(8,128)(2,1)S(1)}, bf16[2,1024,1024]{2,1,0:T(8,128)(2,1)}, u32[]{:S(2)}) copy-start(bf16[2,1024,1024]{2,1,0:T(8,128)(2,1)} %inverse.1) | copy-start | bytes 12582916

commit v2 on v1

v2 whole, which is shorter than its diff:
```python
import jax
import jax.numpy as jnp
from jax import lax
from jax.experimental import pallas as pl
from jax.experimental.pallas import tpu as pltpu
from jax.sharding import PartitionSpec as P

BF = jnp.bfloat16
F32 = jnp.float32
VMEM = pl.BlockSpec(memory_space=pltpu.VMEM)
HBM = pl.BlockSpec(memory_space=pltpu.HBM)
MIB = 1024 * 1024
NT = (((1,), (1,)), ((), ()))


def iota(shape, dim):
    return lax.broadcasted_iota(jnp.int32, shape, dim)


def dot(a, b, dims=(((1,), (0,)), ((), ()))):
    return lax.dot_general(a, b, dims, preferred_element_type=F32)


def send_kernel(
    counts_hbm, currents_hbm, basis_hbm, device_hbm, target_hbm, source_hbm, near_out_hbm, cores_hbm,
    packed, sec_a, sec_b, az_a, az_b, kept, keep,
    counts, currents, basis, device, target_half, source_half, near, cores, sums, staged, sems,
):
    steps, rows = cores.shape[:2]
    pairs = [
        (counts_hbm, counts),
        (currents_hbm, currents),
        (device_hbm, device),
        (target_hbm, target_half),
        (source_hbm, source_half),
        (basis_hbm, basis),
        (near_out_hbm.at[0], near.at[0]),
        (near_out_hbm.at[1], near.at[1]),
    ]
    pairs += [(cores_hbm.at[pl.ds(step * rows, rows)], cores.at[step]) for step in range(steps)]
    copies = [pltpu.make_async_copy(source, to, sems.at[i]) for i, (source, to) in enumerate(pairs)]
    for copy in copies:
        copy.start()
    for copy in copies[:6]:
        copy.wait()

    rank = sec_a.shape[1]
    coeffs = []
    masked = []
    for sub in range(2):
        keep[sub] = (iota(keep.shape[1:], 1) < counts[sub]).astype(F32)
        masked.append(jnp.where(iota(currents.shape[1:], 1) < counts[sub], currents[sub], 0.0).astype(BF))
    for sub in range(2):
        copies[6 + sub].wait()
        coeffs.append(dot(masked[sub], near[sub].reshape(4 * rank, near.shape[3]), NT))
    sec_even, az_even = even("sec"), even("az")
    kept[0] = coeffs[0][:, :rank].astype(BF)
    kept[1] = coeffs[1][:, rank : 2 * rank].astype(BF)
    to_next, to_previous = coeffs[1][:, :rank], coeffs[0][:, rank : 2 * rank]
    sec_a[...] = choose(sec_even, to_next, to_previous)
    sec_b[...] = choose(sec_even, to_previous, to_next)
    for sub in range(2):
        to_next, to_previous = coeffs[sub][:, 2 * rank : 3 * rank], coeffs[sub][:, 3 * rank :]
        az_a[sub] = choose(az_even, to_next, to_previous)
        az_b[sub] = choose(az_even, to_previous, to_next)

    chunks = packed.shape[1] // 2
    lanes = packed.shape[2]
    rhs_count = currents.shape[1]
    far_rank = basis.shape[1]
    width = cores.shape[2] // chunks
    repeat = (iota((rhs_count, lanes), 1) % rhs_count == iota((rhs_count, lanes), 0)).astype(BF)
    diagonal = iota((width, lanes), 0) // far_rank == iota((width, lanes), 1) // rhs_count
    spread = []
    for sub in range(2):
        projected = dot(basis[sub], masked[sub], NT).astype(BF)
        tiled = jnp.concatenate([dot(projected, repeat)] * (width // far_rank), axis=0)
        spread.append(jnp.where(diagonal, tiled, 0.0).astype(BF))

    targets = 2 * packed.shape[0]
    halves = source_half[...] * targets + target_half[...]
    place = halves.reshape(device.shape) + device[...] * 2
    total = None
    for step in range(steps):
        onehot = (iota((2 * targets, rows), 0) == place[:, step * rows : (step + 1) * rows]).astype(BF)
        copies[8 + step].wait()
        term = dot(onehot, cores[step])
        total = term if step == 0 else total + term
    sums[...] = total.astype(BF)
    for k in range(chunks):
        part = pl.ds(k * width, width)
        terms = dot(sums[:targets, part], spread[0]) + dot(sums[targets:, part], spread[1])
        staged[pl.ds(k, targets, stride=chunks), :] = terms
    packed[...] = staged[...].reshape(packed.shape).astype(BF)


def even(axis):
    return lax.rem(lax.axis_index(axis), 2) == 0


def choose(first, yes, no):
    return jnp.where(first, yes.astype(F32), no.astype(F32)).astype(BF)


def solve_kernel(
    keep, right_side, kept, basis, near_hbm, inverse_hbm, base, near_weights, far_weights, near_in, inverse, sems
):
    parts, rows = inverse.shape[1:3]
    copies = [
        pltpu.make_async_copy(inverse_hbm.at[sub, pl.ds(part * rows, rows)], inverse.at[sub, part], sems.at[sub, part])
        for sub in range(2)
        for part in range(parts)
    ]
    near_copies = [pltpu.make_async_copy(near_hbm.at[sub], near_in.at[sub], sems.at[sub, parts]) for sub in range(2)]
    for copy in near_copies[:1] + copies[:parts] + near_copies[1:] + copies[parts:]:
        copy.start()
    rhs_count = right_side.shape[1]
    far_rank = basis.shape[1]
    near_rows = near_weights.shape[1]
    for sub in range(2):
        near_copies[sub].wait()
        rest = jnp.where(keep[sub] > 0.0, right_side[sub], 0.0) - dot(kept[1 - sub], near_in[sub, 1 - sub])
        high = rest.astype(BF)
        low = (rest - high.astype(F32)).astype(BF)
        factors = [near_in[sub, sub], near_in[sub, 2], near_in[sub, 3]]
        stacked = jnp.concatenate(factors + [high, low, basis[sub]], axis=0)
        for part in range(parts):
            copies[sub * parts + part].wait()
            solved = dot(stacked, inverse[sub, part], NT)
            columns = pl.ds(part * rows, rows)
            near_weights[sub, :, columns] = solved[:near_rows].astype(BF)
            rest = solved[near_rows:]
            base[sub, :, columns] = rest[:rhs_count] + rest[rhs_count : 2 * rhs_count]
            far_weights[pl.ds(sub * far_rank, far_rank), columns] = rest[2 * rhs_count :].astype(BF)


def finish_kernel(keep, received, sec_a, sec_b, az_a, az_b, base, near_weights, far_weights, out):
    rhs_count = base.shape[1]
    rank = far_weights.shape[0] // 2
    sums = jnp.sum(received[...].astype(F32), axis=0)
    chunks = sums.shape[0] // 2
    lanes = sums.shape[1]
    own = iota((rhs_count, lanes), 1) % rhs_count == iota((rhs_count, lanes), 0)
    spaced = [jnp.where(own, sums[row : row + 1], 0.0).astype(BF) for row in range(2 * chunks)]
    spaced = [jnp.concatenate(spaced[sub * chunks : (sub + 1) * chunks], axis=1) for sub in range(2)]
    size = (chunks * lanes, 2 * rank)
    select = (iota(size, 0) // rhs_count == iota(size, 1) % rank).astype(BF)
    far_in = dot(jnp.concatenate(spaced, axis=0), select)
    block = iota(far_in.shape, 0) // rhs_count == iota(far_in.shape, 1) // rank
    far_term = dot(jnp.where(block, far_in, 0.0).astype(BF), far_weights[...])

    sec_even, az_even = even("sec"), even("az")
    section = lax.axis_index("sec")
    above = jnp.where(section == 0, 0.0, choose(sec_even, sec_b[...], sec_a[...]).astype(F32))
    below = jnp.where(section == lax.axis_size("sec") - 1, 0.0, choose(sec_even, sec_a[...], sec_b[...]).astype(F32))
    along = [above.astype(BF), below.astype(BF)]
    for sub in range(2):
        west, east = choose(az_even, az_b[sub], az_a[sub]), choose(az_even, az_a[sub], az_b[sub])
        near_term = dot(jnp.concatenate([along[sub], west, east], axis=1), near_weights[sub])
        updated = base[sub] - near_term - far_term[sub * rhs_count : (sub + 1) * rhs_count]
        out[sub] = jnp.where(keep[sub] > 0.0, updated, 0.0)


def swap(value, axis, start):
    sec_count, az_count = lax.axis_size("sec"), lax.axis_size("az")
    route = []
    for sec in range(sec_count):
        for az in range(az_count):
            if axis == "az":
                step = 1 if (az - start) % 2 == 0 else -1
                to = sec, (az + step) % az_count
            else:
                step = 1 if (sec - start) % 2 == 0 else -1
                to = (sec + step, az) if 0 <= sec + step < sec_count else (sec, az ^ 1)
            route.append((sec * az_count + az, to[0] * az_count + to[1]))
    return lax.ppermute(value, ("sec", "az"), route)


def in_hbm(array):
    return pltpu.with_memory_space_constraint(array, pltpu.HBM)


def call(kernel, out_shape, in_specs, flops, moved, grant, scratch=()):
    return pl.pallas_call(
        kernel,
        out_shape=out_shape,
        in_specs=in_specs,
        out_specs=jax.tree.map(lambda _: VMEM, out_shape),
        scratch_shapes=scratch,
        compiler_params=pltpu.CompilerParams(vmem_limit_bytes=grant * MIB),
        cost_estimate=pl.CostEstimate(flops=flops, bytes_accessed=moved, transcendentals=0),
    )


def shape(dims, dtype=BF):
    return jax.ShapeDtypeStruct(dims, dtype)


def local(
    currents,
    right_side,
    counts,
    inverse_blocks,
    near_out,
    near_in,
    far_source_basis,
    far_target_basis,
    far_cores,
    far_target_device,
    far_target_half,
    far_source_half,
):
    _, rhs_count, row_count = currents.shape
    far_rank = far_source_basis.shape[1]
    near_rank = near_out.shape[2]
    far_len = far_cores.shape[0]
    sec_count = lax.axis_size("sec")
    az_count = lax.axis_size("az")
    devices = sec_count * az_count
    width = 256
    chunks = far_cores.shape[1] // width
    lanes = width // far_rank * rhs_count

    piece = shape((rhs_count, near_rank))
    pair = shape((2, rhs_count, near_rank))
    steps = 3
    fetched = [counts, currents, far_source_basis, far_target_device.reshape(1, far_len), far_target_half, far_source_half]
    fetched += [near_out, far_cores]
    packed, sec_a, sec_b, az_a, az_b, kept, keep = call(
        send_kernel,
        (shape((devices, 2 * chunks, lanes)), piece, piece, pair, pair, pair, shape((2, 1, row_count), F32)),
        [HBM] * 8,
        2 * 4 * devices * far_len * row_count,
        2 * (far_cores.size + near_out.size),
        24,
        [
            pltpu.SMEM(counts.shape, jnp.int32),
            pltpu.VMEM(currents.shape, F32),
            pltpu.VMEM(far_source_basis.shape, BF),
            pltpu.VMEM((1, far_len), jnp.int32),
            pltpu.VMEM((far_len,), jnp.int32),
            pltpu.VMEM((far_len,), jnp.int32),
            pltpu.VMEM(near_out.shape, BF),
            pltpu.VMEM((steps, far_len // steps, far_cores.shape[1]), BF),
            pltpu.VMEM((4 * devices, far_cores.shape[1]), BF),
            pltpu.VMEM((2 * devices * chunks, lanes), F32),
            pltpu.SemaphoreType.DMA((8 + steps,)),
        ],
    )(*[in_hbm(x) for x in fetched])
    received = lax.all_to_all(packed, ("sec", "az"), split_axis=0, concat_axis=0, tiled=True)
    sec_a, sec_b = swap(sec_a, "sec", 0), swap(sec_b, "sec", 1)
    az_a, az_b = swap(az_a, "az", 0), swap(az_b, "az", 1)

    parts = 2
    base, near_weights, far_weights = call(
        solve_kernel,
        (
            shape((2, rhs_count, row_count), F32),
            shape((2, 3 * near_rank, row_count)),
            shape((2 * far_rank, row_count)),
        ),
        [VMEM] * 4 + [HBM] * 2,
        2 * inverse_blocks.size * (3 * near_rank + 2 * rhs_count + far_rank),
        inverse_blocks.size * 2,
        16,
        [
            pltpu.VMEM(near_in.shape, BF),
            pltpu.VMEM((2, parts, row_count // parts, row_count), BF),
            pltpu.SemaphoreType.DMA((2, parts + 1)),
        ],
    )(keep, right_side, kept, far_target_basis, in_hbm(near_in), in_hbm(inverse_blocks))

    return call(
        finish_kernel,
        shape((2, rhs_count, row_count), F32),
        [VMEM] * 9,
        2 * 2 * rhs_count * (3 * near_rank + far_rank) * row_count,
        received.size * 2,
        4,
    )(keep, received, sec_a, sec_b, az_a, az_b, base, near_weights, far_weights)


def solution(mesh):
    in_specs = (
        P(("sec", "az"), None, None),
        P(("sec", "az"), None, None),
        P(("sec", "az")),
        P(("sec", "az"), None, None),
        P(("sec", "az"), None, None, None),
        P(("sec", "az"), None, None, None),
        P(("sec", "az"), None, None),
        P(("sec", "az"), None, None),
        P(("sec", "az"), None),
        P(("sec", "az"), None),
        P(("sec", "az")),
        P(("sec", "az")),
    )
    out_specs = P(("sec", "az"), None, None)
    return jax.shard_map(local, mesh=mesh, in_specs=in_specs, out_specs=out_specs, check_vma=False)
```

time: 45.9 us -> 29.8 us (0.65)
  the two profiles are of different devices: /device:TPU:6 before, /device:TPU:1 now
where the time goes in v2:
time: 29.8 us; the launch traced here: 29.7 us
  starting transfers between devices  15.2 us (51%)
  Pallas kernels  11.6 us (39%)
  waiting for transfers between devices  2.79 us (9%)
    all_to_all x1, starting transfers between devices, local(): lax.all_to_all(packed, ('sec', 'az'), split_axis=0, concat_axis=0, tiled=...  11.5 us
    pallas_call x1, Pallas kernels, local(): call(send_kernel, (shape((devices, 2 * chunks, lanes)), piece, piece, pai...  5.81 us
    pallas_call x1, Pallas kernels, local(): call(solve_kernel, (shape((2, rhs_count, row_count), F32), shape((2, 3 *...  4.56 us
    ppermute x4, starting transfers between devices, swap(): return lax.ppermute(value, ('sec', 'az'), route)  3.69 us
    all_to_all x1, waiting for transfers between devices, local(): lax.all_to_all(packed, ('sec', 'az'), split_axis=0, concat_axis=0, tiled=...  2.78 us
    pallas_call x1, Pallas kernels, local(): call(finish_kernel, shape((2, rhs_count, row_count), F32), [VMEM] * 9, 2...  1.28 us
  transfers between devices with their start and end apart: 5, of which 1 were waited for; matrix products, arithmetic and copies ran while one was open for 0% of the time, Pallas kernels for 15%

profile of v2, /device:TPU:1, one launch (start us, length us, event | category | flops | bytes accessed | tf_op | source)
XLA Modules:
  0.0 29.7 jit_solution(14828624452108587351)
XLA Ops:
  0.0 0.0 copy-start
  0.0 0.0 copy-start.1
  0.0 5.8 %shard_map.118 = (bf16[128,8,128]{2,1,0:T(8,128)(2,1)}, bf16[16,128]{1,0:T(8,128)(2,1)S(1)}, bf16[16,128]{1,0:T(8,128)(2,1)S(1)}, bf16[2,16,128]{2,1,0:T(8,128)(...) custom-call(s32[2]{0:T(128)} %counts_hbm.1, ...), custom_call_target="tpu_custom_call" | custom-call | flops 1610612736 | bytes 5242880 | tf_op jit(solution)/shard_map/pallas_call | solution.py:229
  5.8 11.5 %all-to-all-start = ((bf16[128,8,128]{2,1,0:T(8,128)(2,1)}), bf16[128,8,128]{2,1,0:T(8,128)(2,1)S(1)}, u32[]{:S(2)}, u32[]{:S(2)}) async-start(bf16[128,8,128]{2,1,0:T(8,128)(2,1)} %get-tuple-element.16), calls=%async_computation | async-start | bytes 524288 | tf_op jit(solution)/shard_map/all_to_all | solution.py:250
  17.3 1.5 %collective-permute-start = (bf16[16,128]{1,0:T(8,128)(2,1)S(1)}, bf16[16,128]{1,0:T(8,128)(2,1)S(1)}, u32[]{:S(2)}, u32[]{:S(2)}) collective-permute-start(bf16[16,128]{1,0:T(8,128)(2,1)S(1)} %get-tuple-element.17), channel_id=1, source_target_pairs={{0,8},{1,9},{2,10},{3,11},{4,12},{5,13},{6,14},{7,15},{8,0},{9,1},... | collective-permute-start | bytes 12296 | tf_op jit(solution)/shard_map/ppermute | solution.py:176
  18.8 0.6 %collective-permute-start.1 = (bf16[16,128]{1,0:T(8,128)(2,1)S(1)}, bf16[16,128]{1,0:T(8,128)(2,1)S(1)}, u32[]{:S(2)}, u32[]{:S(2)}) collective-permute-start(bf16[16,128]{1,0:T(8,128)(2,1)S(1)} %get-tuple-element.18), channel_id=1, source_target_pairs={{0,1},{1,0},{2,3},{3,2},{4,5},{5,4},{6,7},{7,6},{8,16},{9,17},{10,... | collective-permute-start | bytes 12296 | tf_op jit(solution)/shard_map/ppermute | solution.py:176
  19.4 0.0 collective-permute-start.2
  19.4 1.6 %collective-permute-start.3 = (bf16[2,16,128]{2,1,0:T(8,128)(2,1)S(1)}, bf16[2,16,128]{2,1,0:T(8,128)(2,1)S(1)}, u32[]{:S(2)}, u32[]{:S(2)}) collective-permute-start(bf16[2,16,128]{2,1,0:T(8,128)(2,1)S(1)} %get-tuple-element.20), channel_id=1, source_target_pairs={{0,7},{1,2},{2,1},{3,4},{4,3},{5,6},{6,5},{7,0},{8,15},{9,10},{10,... | collective-permute-start | bytes 24584 | tf_op jit(solution)/shard_map/ppermute | solution.py:176
  21.0 0.0 copy-done
  21.0 0.0 copy-done.1
  21.0 4.6 %shard_map.119 = (f32[2,16,1024]{2,1,0:T(8,128)S(1)}, bf16[2,384,1024]{2,1,0:T(8,128)(2,1)S(1)}, bf16[64,1024]{1,0:T(8,128)(2,1)S(1)}) custom-call(f32[2,1,1024]{2,1,0:T(1,128)S(1)} %get-tuple-element.15.keep, f32[2,16,1024]{2,1,0:T(8,128)S(1)} %copy-done, bf16[2,16,128]{2,1,0:T(8,128)(2,1)S(1)} %get-tuple-element.21.kept, ...), custom_call_target="tpu_custom_call" | custom-call | flops 1879048192 | bytes 4194304 | tf_op jit(solution)/shard_map/pallas_call | solution.py:255
  25.6 0.0 collective-permute-done.sec_a
  25.6 0.0 collective-permute-done.1.sec_b
  25.6 0.0 collective-permute-done.2.az_a
  25.6 0.0 collective-permute-done.3.az_b
  25.6 2.8 %all-to-all-done.received = bf16[128,8,128]{2,1,0:T(8,128)(2,1)S(1)} async-done(((bf16[128,8,128]{2,1,0:T(8,128)(2,1)}), bf16[128,8,128]{2,1,0:T(8,128)(2,1)S(1)}, u32[]{:S(2)}, u32[]{:S(2)}) %all-to-all-start) | async-done | bytes 262176 | tf_op jit(solution)/shard_map/all_to_all | solution.py:250
  28.4 1.3 %shard_map.120 = f32[2,16,1024]{2,1,0:T(8,128)} custom-call(f32[2,1,1024]{2,1,0:T(1,128)S(1)} %get-tuple-element.15.keep, bf16[128,8,128]{2,1,0:T(8,128)(2,1)S(1)} %all-to-all-done.received, bf16[16,128]{1,0:T(8,128)(2,1)S(1)} %collective-permute-done.sec_a, bf16[16,128]{1,0:T(8,128)(2,1)S(1)} %collective-permute-done.1.sec_b, ...), custom_call_target="tpu_custom_call" | custom-call | flops 27262976 | bytes 262144 | tf_op jit(solution)/shard_map/pallas_call | solution.py:273
Async XLA Ops:
  0.0 21.0 %copy-start = (f32[2,16,1024]{2,1,0:T(8,128)S(1)}, f32[2,16,1024]{2,1,0:T(8,128)}, u32[]{:S(2)}) copy-start(f32[2,16,1024]{2,1,0:T(8,128)} %right_side.1) | copy-start | bytes 393220
  0.0 21.0 %copy-start.1 = (bf16[2,32,1024]{2,1,0:T(8,128)(2,1)S(1)}, bf16[2,32,1024]{2,1,0:T(8,128)(2,1)}, u32[]{:S(2)}) copy-start(bf16[2,32,1024]{2,1,0:T(8,128)(2,1)} %basis.1) | copy-start | bytes 393220
  5.8 22.6 %all-to-all-start = ((bf16[128,8,128]{2,1,0:T(8,128)(2,1)}), bf16[128,8,128]{2,1,0:T(8,128)(2,1)S(1)}, u32[]{:S(2)}, u32[]{:S(2)}) async-start(bf16[128,8,128]{2,1,0:T(8,128)(2,1)} %get-tuple-element.16), calls=%async_computation | async-start | bytes 524288 | tf_op jit(solution)/shard_map/all_to_all | solution.py:250
  17.3 8.3 %collective-permute-start = (bf16[16,128]{1,0:T(8,128)(2,1)S(1)}, bf16[16,128]{1,0:T(8,128)(2,1)S(1)}, u32[]{:S(2)}, u32[]{:S(2)}) collective-permute-start(bf16[16,128]{1,0:T(8,128)(2,1)S(1)} %get-tuple-element.17), channel_id=1, source_target_pairs={{0,8},{1,9},{2,10},{3,11},{4,12},{5,13},{6,14},{7,15},{8,0},{9,1},... | collective-permute-start | bytes 12296 | tf_op jit(solution)/shard_map/ppermute | solution.py:176
  18.8 6.8 %collective-permute-start.1 = (bf16[16,128]{1,0:T(8,128)(2,1)S(1)}, bf16[16,128]{1,0:T(8,128)(2,1)S(1)}, u32[]{:S(2)}, u32[]{:S(2)}) collective-permute-start(bf16[16,128]{1,0:T(8,128)(2,1)S(1)} %get-tuple-element.18), channel_id=1, source_target_pairs={{0,1},{1,0},{2,3},{3,2},{4,5},{5,4},{6,7},{7,6},{8,16},{9,17},{10,... | collective-permute-start | bytes 12296 | tf_op jit(solution)/shard_map/ppermute | solution.py:176
  19.4 6.2 %collective-permute-start.2 = (bf16[2,16,128]{2,1,0:T(8,128)(2,1)S(1)}, bf16[2,16,128]{2,1,0:T(8,128)(2,1)S(1)}, u32[]{:S(2)}, u32[]{:S(2)}) collective-permute-start(bf16[2,16,128]{2,1,0:T(8,128)(2,1)S(1)} %get-tuple-element.19), channel_id=1, source_target_pairs={{0,1},{1,0},{2,3},{3,2},{4,5},{5,4},{6,7},{7,6},{8,9},{9,8},{10,11... | collective-permute-start | bytes 24584 | tf_op jit(solution)/shard_map/ppermute | solution.py:176
  19.4 6.2 %collective-permute-start.3 = (bf16[2,16,128]{2,1,0:T(8,128)(2,1)S(1)}, bf16[2,16,128]{2,1,0:T(8,128)(2,1)S(1)}, u32[]{:S(2)}, u32[]{:S(2)}) collective-permute-start(bf16[2,16,128]{2,1,0:T(8,128)(2,1)S(1)} %get-tuple-element.20), channel_id=1, source_target_pairs={{0,7},{1,2},{2,1},{3,4},{4,3},{5,6},{6,5},{7,0},{8,15},{9,10},{10,... | collective-permute-start | bytes 24584 | tf_op jit(solution)/shard_map/ppermute | solution.py:176

commit v3 on v2

v3 whole, which is shorter than its diff:
```python
import jax
import jax.numpy as jnp
from jax import lax
from jax.experimental import pallas as pl
from jax.experimental.pallas import tpu as pltpu
from jax.sharding import PartitionSpec as P

BF = jnp.bfloat16
F32 = jnp.float32
VMEM = pl.BlockSpec(memory_space=pltpu.VMEM)
HBM = pl.BlockSpec(memory_space=pltpu.HBM)
MIB = 1024 * 1024
NT = (((1,), (1,)), ((), ()))


def iota(shape, dim):
    return lax.broadcasted_iota(jnp.int32, shape, dim)


def dot(a, b, dims=(((1,), (0,)), ((), ()))):
    return lax.dot_general(a, b, dims, preferred_element_type=F32)


def far_out_kernel(
    counts_hbm, currents_hbm, basis_hbm, device_hbm, target_hbm, source_hbm, cores_hbm,
    packed, masked, keep,
    counts, currents, basis, device, target_half, source_half, cores, terms, staged, sems,
):
    steps, rows = cores.shape[:2]
    pairs = [
        (counts_hbm, counts),
        (currents_hbm, currents),
        (basis_hbm, basis),
        (device_hbm, device),
        (target_hbm, target_half),
        (source_hbm, source_half),
    ]
    pairs += [(cores_hbm.at[pl.ds(step * rows, rows)], cores.at[step]) for step in range(steps)]
    copies = [pltpu.make_async_copy(source, to, sems.at[i]) for i, (source, to) in enumerate(pairs)]
    for copy in copies:
        copy.start()
    for copy in copies[:6]:
        copy.wait()

    chunks = packed.shape[1] // 2
    lanes = packed.shape[2]
    rhs_count = currents.shape[1]
    far_rank = basis.shape[1]
    width = cores.shape[2] // chunks
    targets = 2 * packed.shape[0]

    for sub in range(2):
        keep[sub] = (iota(keep.shape[1:], 1) < counts[sub]).astype(F32)
        masked[sub] = jnp.where(iota(currents.shape[1:], 1) < counts[sub], currents[sub], 0.0).astype(BF)
    both_masked = jnp.concatenate([masked[0], masked[1]], axis=0)
    projected = [dot(basis[sub], both_masked, NT).astype(BF) for sub in range(2)]
    size = (2 * rhs_count, 2 * lanes)
    repeat = iota(size, 1) // lanes * rhs_count + iota(size, 1) % rhs_count == iota(size, 0)
    repeat = repeat.astype(BF)
    size = (width, 2 * lanes)
    diagonal = iota(size, 0) // far_rank == iota(size, 1) % lanes // rhs_count
    tiled = [dot(projected[sub], repeat)[:, sub * lanes : (sub + 1) * lanes] for sub in range(2)]
    tiled = jnp.concatenate([jnp.concatenate(tiled, axis=1)] * (width // far_rank), axis=0)
    spread = jnp.where(diagonal, tiled, 0.0).astype(BF)

    source = source_half[...].reshape(device.shape).astype(F32)
    count = device.shape[1]
    second = [
        jnp.broadcast_to(source[:, start : start + lanes], (lanes, lanes)).T > 0.5 for start in range(0, count, lanes)
    ]
    target = device[...] * 2 + target_half[...].reshape(device.shape)
    onehot = (iota((targets, count), 0) == target).astype(BF)

    sums = None
    for step in range(steps + 1):
        if step < steps:
            copies[6 + step].wait()
            for k in range(chunks):
                both = dot(cores[step, :, k * width : (k + 1) * width], spread)
                for part in range(rows // lanes):
                    piece = both[part * lanes : (part + 1) * lanes]
                    chosen = jnp.where(second[step * (rows // lanes) + part], piece[:, lanes:], piece[:, :lanes])
                    terms[pl.ds(step * rows + part * lanes, lanes), pl.ds(k * lanes, lanes)] = chosen.astype(BF)
        if step > 0:
            part = slice((step - 1) * rows, step * rows)
            term = dot(onehot[:, part], terms[part, :])
            sums = term if sums is None else sums + term
    for k in range(chunks):
        staged[pl.ds(k, targets, stride=chunks), :] = sums[:, k * lanes : (k + 1) * lanes]
    packed[...] = staged[...].reshape(packed.shape).astype(BF)


def even(axis):
    return lax.rem(lax.axis_index(axis), 2) == 0


def choose(first, yes, no):
    return jnp.where(first, yes.astype(F32), no.astype(F32)).astype(BF)


def near_out_kernel(masked, near, sec_a, sec_b, az_a, az_b, kept):
    rank = sec_a.shape[1]
    sec_even, az_even = even("sec"), even("az")
    coeffs = []
    for sub in range(2):
        coeffs.append(dot(masked[sub], near[sub].reshape(4 * rank, near.shape[3]), NT))
    kept[0] = coeffs[0][:, :rank].astype(BF)
    kept[1] = coeffs[1][:, rank : 2 * rank].astype(BF)
    to_next, to_previous = coeffs[1][:, :rank], coeffs[0][:, rank : 2 * rank]
    sec_a[...] = choose(sec_even, to_next, to_previous)
    sec_b[...] = choose(sec_even, to_previous, to_next)
    for sub in range(2):
        to_next, to_previous = coeffs[sub][:, 2 * rank : 3 * rank], coeffs[sub][:, 3 * rank :]
        az_a[sub] = choose(az_even, to_next, to_previous)
        az_b[sub] = choose(az_even, to_previous, to_next)


def solve_kernel(
    keep, right_side, kept, basis, near_in, inverse_hbm, base, near_weights, far_weights, inverse, sems
):
    parts, rows = inverse.shape[1:3]
    copies = [
        pltpu.make_async_copy(inverse_hbm.at[sub, pl.ds(part * rows, rows)], inverse.at[sub, part], sems.at[sub, part])
        for sub in range(2)
        for part in range(parts)
    ]
    for copy in copies:
        copy.start()
    rhs_count = right_side.shape[1]
    far_rank = basis.shape[1]
    near_rows = near_weights.shape[1]
    for sub in range(2):
        rest = jnp.where(keep[sub] > 0.0, right_side[sub], 0.0) - dot(kept[1 - sub], near_in[sub, 1 - sub])
        high = rest.astype(BF)
        low = (rest - high.astype(F32)).astype(BF)
        factors = [near_in[sub, sub], near_in[sub, 2], near_in[sub, 3]]
        stacked = jnp.concatenate(factors + [high, low, basis[sub]], axis=0)
        for part in range(parts):
            copies[sub * parts + part].wait()
            solved = dot(stacked, inverse[sub, part], NT)
            columns = pl.ds(part * rows, rows)
            near_weights[sub, :, columns] = solved[:near_rows].astype(BF)
            rest = solved[near_rows:]
            base[sub, :, columns] = rest[:rhs_count] + rest[rhs_count : 2 * rhs_count]
            rest = jnp.where(keep[sub, :, part * rows : (part + 1) * rows] > 0.0, rest[2 * rhs_count :], 0.0)
            far_weights[pl.ds(sub * far_rank, far_rank), columns] = rest.astype(BF)


def near_in_kernel(keep, sec_a, sec_b, az_a, az_b, base, near_weights, solved):
    sec_even, az_even = even("sec"), even("az")
    section = lax.axis_index("sec")
    above = jnp.where(section == 0, 0.0, choose(sec_even, sec_b[...], sec_a[...]).astype(F32))
    below = jnp.where(section == lax.axis_size("sec") - 1, 0.0, choose(sec_even, sec_a[...], sec_b[...]).astype(F32))
    along = [above.astype(BF), below.astype(BF)]
    for sub in range(2):
        west, east = choose(az_even, az_b[sub], az_a[sub]), choose(az_even, az_a[sub], az_b[sub])
        near_term = dot(jnp.concatenate([along[sub], west, east], axis=1), near_weights[sub])
        solved[sub] = jnp.where(keep[sub] > 0.0, base[sub] - near_term, 0.0)


def far_in_kernel(received, solved, far_weights, out):
    rhs_count = solved.shape[1]
    rank = far_weights.shape[0] // 2
    sums = jnp.sum(received[...].astype(F32), axis=0)
    chunks = sums.shape[0] // 2
    lanes = sums.shape[1]
    own = iota((rhs_count, lanes), 1) % rhs_count == iota((rhs_count, lanes), 0)
    spaced = [jnp.where(own, sums[row : row + 1], 0.0).astype(BF) for row in range(2 * chunks)]
    spaced = [jnp.concatenate(spaced[sub * chunks : (sub + 1) * chunks], axis=1) for sub in range(2)]
    size = (chunks * lanes, 2 * rank)
    select = (iota(size, 0) // rhs_count == iota(size, 1) % rank).astype(BF)
    far_in = dot(jnp.concatenate(spaced, axis=0), select)
    block = iota(far_in.shape, 0) // rhs_count == iota(far_in.shape, 1) // rank
    far_term = dot(jnp.where(block, far_in, 0.0).astype(BF), far_weights[...])
    for sub in range(2):
        out[sub] = solved[sub] - far_term[sub * rhs_count : (sub + 1) * rhs_count]


def swap(value, axis, start):
    sec_count, az_count = lax.axis_size("sec"), lax.axis_size("az")
    route = []
    for sec in range(sec_count):
        for az in range(az_count):
            if axis == "az":
                step = 1 if (az - start) % 2 == 0 else -1
                to = sec, (az + step) % az_count
            else:
                step = 1 if (sec - start) % 2 == 0 else -1
                to = (sec + step, az) if 0 <= sec + step < sec_count else (sec, az ^ 1)
            route.append((sec * az_count + az, to[0] * az_count + to[1]))
    return lax.ppermute(value, ("sec", "az"), route)


def in_hbm(array):
    return pltpu.with_memory_space_constraint(array, pltpu.HBM)


def call(kernel, out_shape, in_specs, flops, moved, grant, scratch=()):
    return pl.pallas_call(
        kernel,
        out_shape=out_shape,
        in_specs=in_specs,
        out_specs=jax.tree.map(lambda _: VMEM, out_shape),
        scratch_shapes=scratch,
        compiler_params=pltpu.CompilerParams(vmem_limit_bytes=grant * MIB),
        cost_estimate=pl.CostEstimate(flops=flops, bytes_accessed=moved, transcendentals=0),
    )


def shape(dims, dtype=BF):
    return jax.ShapeDtypeStruct(dims, dtype)


def local(
    currents,
    right_side,
    counts,
    inverse_blocks,
    near_out,
    near_in,
    far_source_basis,
    far_target_basis,
    far_cores,
    far_target_device,
    far_target_half,
    far_source_half,
):
    _, rhs_count, row_count = currents.shape
    far_rank = far_source_basis.shape[1]
    near_rank = near_out.shape[2]
    far_len = far_cores.shape[0]
    sec_count = lax.axis_size("sec")
    az_count = lax.axis_size("az")
    devices = sec_count * az_count
    width = 256
    chunks = far_cores.shape[1] // width
    lanes = width // far_rank * rhs_count

    piece = shape((rhs_count, near_rank))
    pair = shape((2, rhs_count, near_rank))
    steps = 3
    fetched = [counts, currents, far_source_basis, far_target_device.reshape(1, far_len), far_target_half, far_source_half]
    packed, masked, keep = call(
        far_out_kernel,
        (shape((devices, 2 * chunks, lanes)), shape(currents.shape), shape((2, 1, row_count), F32)),
        [HBM] * 7,
        2 * 2 * devices * far_len * row_count,
        2 * far_cores.size,
        20,
        [
            pltpu.SMEM(counts.shape, jnp.int32),
            pltpu.VMEM(currents.shape, F32),
            pltpu.VMEM(far_source_basis.shape, BF),
            pltpu.VMEM((1, far_len), jnp.int32),
            pltpu.VMEM((far_len,), jnp.int32),
            pltpu.VMEM((far_len,), jnp.int32),
            pltpu.VMEM((steps, far_len // steps, far_cores.shape[1]), BF),
            pltpu.VMEM((far_len, chunks * lanes), BF),
            pltpu.VMEM((2 * devices * chunks, lanes), F32),
            pltpu.SemaphoreType.DMA((6 + steps,)),
        ],
    )(*[in_hbm(x) for x in fetched + [far_cores]])
    received = lax.all_to_all(packed, ("sec", "az"), split_axis=0, concat_axis=0, tiled=True)

    sec_a, sec_b, az_a, az_b, kept = call(
        near_out_kernel,
        (piece, piece, pair, pair, pair),
        [VMEM] * 2,
        2 * near_out.size * rhs_count,
        near_out.size * 2,
        2,
    )(masked, near_out)
    sec_a, sec_b = swap(sec_a, "sec", 0), swap(sec_b, "sec", 1)
    az_a, az_b = swap(az_a, "az", 0), swap(az_b, "az", 1)

    parts = 2
    base, near_weights, far_weights = call(
        solve_kernel,
        (
            shape((2, rhs_count, row_count), F32),
            shape((2, 3 * near_rank, row_count)),
            shape((2 * far_rank, row_count)),
        ),
        [VMEM] * 5 + [HBM],
        2 * inverse_blocks.size * (3 * near_rank + 2 * rhs_count + far_rank),
        inverse_blocks.size * 2,
        16,
        [
            pltpu.VMEM((2, parts, row_count // parts, row_count), BF),
            pltpu.SemaphoreType.DMA((2, parts)),
        ],
    )(keep, right_side, kept, far_target_basis, near_in, in_hbm(inverse_blocks))

    solved = call(
        near_in_kernel,
        shape(right_side.shape, F32),
        [VMEM] * 7,
        2 * 2 * rhs_count * 3 * near_rank * row_count,
        2 * near_in.size,
        4,
    )(keep, sec_a, sec_b, az_a, az_b, base, near_weights)

    return call(
        far_in_kernel,
        shape(right_side.shape, F32),
        [VMEM] * 3,
        2 * 2 * rhs_count * far_rank * row_count,
        received.size * 2,
        4,
    )(received, solved, far_weights)


def solution(mesh):
    in_specs = (
        P(("sec", "az"), None, None),
        P(("sec", "az"), None, None),
        P(("sec", "az")),
        P(("sec", "az"), None, None),
        P(("sec", "az"), None, None, None),
        P(("sec", "az"), None, None, None),
        P(("sec", "az"), None, None),
        P(("sec", "az"), None, None),
        P(("sec", "az"), None),
        P(("sec", "az"), None),
        P(("sec", "az")),
        P(("sec", "az")),
    )
    out_specs = P(("sec", "az"), None, None)
    return jax.shard_map(local, mesh=mesh, in_specs=in_specs, out_specs=out_specs, check_vma=False)
```

time: 29.8 us -> 28 us (0.940)
  Pallas kernels: 11.6 us -> 10.2 us
  waiting for transfers between devices: 2.79 us -> 2.32 us
    pallas_call x2 -> x4, Pallas kernels: 7.09 us -> 6.15 us  [the longest x1 4.11 us: local(): call(far_out_kernel, (shape((devices, 2 * chunks, lanes)), shape(currents...]
    all_to_all x1, waiting for transfers between devices: 2.78 us -> 2.31 us  [local(): lax.all_to_all(packed, ('sec', 'az'), split_axis=0, concat_axis=0, tiled=...]
    pallas_call x1, Pallas kernels: 4.56 us -> 4.1 us  [local(): call(solve_kernel, (shape((2, rhs_count, row_count), F32), shape((2, 3 *...]
  transfers between devices with their start and end apart: 5 -> 5, of which waited for: 1 -> 1; matrix products, arithmetic and copies ran while one was open for 0% -> 0% of each run, Pallas kernels for 15% -> 18%
where the time goes in v3:
time: 28 us; the launch traced here: 27.8 us
  starting transfers between devices  15.1 us (54%)
  Pallas kernels  10.2 us (36%)
  waiting for transfers between devices  2.32 us (8%)
    all_to_all x1, starting transfers between devices, local(): lax.all_to_all(packed, ('sec', 'az'), split_axis=0, concat_axis=0, tiled=...  11.5 us
    pallas_call x1, Pallas kernels, local(): call(far_out_kernel, (shape((devices, 2 * chunks, lanes)), shape(currents...  4.11 us
    pallas_call x1, Pallas kernels, local(): call(solve_kernel, (shape((2, rhs_count, row_count), F32), shape((2, 3 *...  4.1 us
    ppermute x4, starting transfers between devices, swap(): return lax.ppermute(value, ('sec', 'az'), route)  3.62 us
    all_to_all x1, waiting for transfers between devices, local(): lax.all_to_all(packed, ('sec', 'az'), split_axis=0, concat_axis=0, tiled=...  2.31 us
    pallas_call x1, Pallas kernels, local(): call(far_in_kernel, shape(right_side.shape, F32), [VMEM] * 3, 2 * 2 * rhs...  1.07 us
    pallas_call x1, Pallas kernels, local(): call(near_out_kernel, (piece, piece, pair, pair, pair), [VMEM] * 2, 2 * n...  0.65 us
  transfers between devices with their start and end apart: 5, of which 1 were waited for; matrix products, arithmetic and copies ran while one was open for 0% of the time, Pallas kernels for 18%

profile of v3, /device:TPU:1, one launch (start us, length us, event | category | flops | bytes accessed | tf_op | source)
XLA Modules:
  0.0 27.8 jit_solution(588449121978507474)
XLA Ops:
  0.0 0.0 copy-start
  0.0 4.1 %shard_map.118 = (bf16[128,8,128]{2,1,0:T(8,128)(2,1)}, bf16[2,16,1024]{2,1,0:T(8,128)(2,1)S(1)}, f32[2,1,1024]{2,1,0:T(1,128)S(1)}) custom-call(s32[2]{0:T(128)} %counts_hbm.1, f32[2,16,1024]{2,1,0:T(8,128)} %currents_hbm.1, bf16[2,32,1024]{2,1,0:T(8,128)(2,1)} %basis_hbm.1, s32[1,1536]{1,0:T(1,128)} %bitcast.1, s32[1536]{0:T(1024)} %target_hbm.1, ...), custom_call_target="tpu_custom_call" | custom-call | flops 805306368 | bytes 3145728 | tf_op jit(solution)/shard_map/pallas_call | solution.py:243
  4.1 0.0 copy-start.2
  4.1 0.0 copy-start.3
  4.1 11.5 %all-to-all-start = ((bf16[128,8,128]{2,1,0:T(8,128)(2,1)}), bf16[128,8,128]{2,1,0:T(8,128)(2,1)S(1)}, u32[]{:S(2)}, u32[]{:S(2)}) async-start(bf16[128,8,128]{2,1,0:T(8,128)(2,1)} %get-tuple-element.16), calls=%async_computation | async-start | bytes 524288 | tf_op jit(solution)/shard_map/all_to_all | solution.py:263
  15.7 0.0 copy-start.1
  15.7 0.0 copy-done
  15.7 0.6 %shard_map.119 = (bf16[16,128]{1,0:T(8,128)(2,1)S(1)}, bf16[16,128]{1,0:T(8,128)(2,1)S(1)}, bf16[2,16,128]{2,1,0:T(8,128)(2,1)S(1)}, bf16[2,16,128]{2,1,0:T(8,128)(2,1)S(1)}, bf16[2,16,128]{2,1,0:T(8,128)(2,1)S(1)}) custom-call(bf16[2,16,1024]{2,1,0:T(8,128)(2,1)S(1)} %get-tuple-element.18.masked, bf16[2,4,128,1024]{3,2,1,0:T(8,128)(2,1)S(1)} %copy-done), custom_call_target="tpu_custom_call" | custom-call | flops 33554432 | bytes 2097152 | tf_op jit(solution)/shard_map/pallas_call | solution.py:265
  16.3 1.4 %collective-permute-start = (bf16[16,128]{1,0:T(8,128)(2,1)S(1)}, bf16[16,128]{1,0:T(8,128)(2,1)S(1)}, u32[]{:S(2)}, u32[]{:S(2)}) collective-permute-start(bf16[16,128]{1,0:T(8,128)(2,1)S(1)} %get-tuple-element.19), channel_id=1, source_target_pairs={{0,8},{1,9},{2,10},{3,11},{4,12},{5,13},{6,14},{7,15},{8,0},{9,1},... | collective-permute-start | bytes 12296 | tf_op jit(solution)/shard_map/ppermute | solution.py:191
  17.7 0.6 %collective-permute-start.1 = (bf16[16,128]{1,0:T(8,128)(2,1)S(1)}, bf16[16,128]{1,0:T(8,128)(2,1)S(1)}, u32[]{:S(2)}, u32[]{:S(2)}) collective-permute-start(bf16[16,128]{1,0:T(8,128)(2,1)S(1)} %get-tuple-element.20), channel_id=1, source_target_pairs={{0,1},{1,0},{2,3},{3,2},{4,5},{5,4},{6,7},{7,6},{8,16},{9,17},{10,... | collective-permute-start | bytes 12296 | tf_op jit(solution)/shard_map/ppermute | solution.py:191
  18.4 0.0 collective-permute-start.2
  18.4 1.6 %collective-permute-start.3 = (bf16[2,16,128]{2,1,0:T(8,128)(2,1)S(1)}, bf16[2,16,128]{2,1,0:T(8,128)(2,1)S(1)}, u32[]{:S(2)}, u32[]{:S(2)}) collective-permute-start(bf16[2,16,128]{2,1,0:T(8,128)(2,1)S(1)} %get-tuple-element.22), channel_id=1, source_target_pairs={{0,7},{1,2},{2,1},{3,4},{4,3},{5,6},{6,5},{7,0},{8,15},{9,10},{10,... | collective-permute-start | bytes 24584 | tf_op jit(solution)/shard_map/ppermute | solution.py:191
  20.0 0.0 copy-done.2
  20.0 0.0 copy-done.3
  20.0 0.0 copy-done.1
  20.0 4.1 %shard_map.120 = (f32[2,16,1024]{2,1,0:T(8,128)S(1)}, bf16[2,384,1024]{2,1,0:T(8,128)(2,1)S(1)}, bf16[64,1024]{1,0:T(8,128)(2,1)S(1)}) custom-call(f32[2,1,1024]{2,1,0:T(1,128)S(1)} %get-tuple-element.17.keep, f32[2,16,1024]{2,1,0:T(8,128)S(1)} %copy-done.2, bf16[2,16,128]{2,1,0:T(8,128)(2,1)S(1)} %get-tuple-element.23.kept, ...), custom_call_target="tpu_custom_call" | custom-call | flops 1879048192 | bytes 4194304 | tf_op jit(solution)/shard_map/pallas_call | solution.py:277
  24.1 0.0 collective-permute-done.sec_a
  24.1 0.0 collective-permute-done.1.sec_b
  24.1 0.0 collective-permute-done.2.az_a
  24.1 0.0 collective-permute-done.3.az_b
  24.1 0.3 %shard_map.121.solved = f32[2,16,1024]{2,1,0:T(8,128)S(1)} custom-call(f32[2,1,1024]{2,1,0:T(1,128)S(1)} %get-tuple-element.17.keep, bf16[16,128]{1,0:T(8,128)(2,1)S(1)} %collective-permute-done.sec_a, bf16[16,128]{1,0:T(8,128)(2,1)S(1)} %collective-permute-done.1.sec_b, bf16[2,16,128]{2,1,0:T(8,128)(2,1)S(1)} %collective-permute-done.2.az_a, ...), custom_call_target="tpu_custom_call" | custom-call | flops 25165824 | bytes 2097152 | tf_op jit(solution)/shard_map/pallas_call | solution.py:294
  24.4 2.3 %all-to-all-done.received = bf16[128,8,128]{2,1,0:T(8,128)(2,1)S(1)} async-done(((bf16[128,8,128]{2,1,0:T(8,128)(2,1)}), bf16[128,8,128]{2,1,0:T(8,128)(2,1)S(1)}, u32[]{:S(2)}, u32[]{:S(2)}) %all-to-all-start) | async-done | bytes 262176 | tf_op jit(solution)/shard_map/all_to_all | solution.py:263
  26.7 1.1 %shard_map.122 = f32[2,16,1024]{2,1,0:T(8,128)} custom-call(bf16[128,8,128]{2,1,0:T(8,128)(2,1)S(1)} %all-to-all-done.received, f32[2,16,1024]{2,1,0:T(8,128)S(1)} %shard_map.121.solved, bf16[64,1024]{1,0:T(8,128)(2,1)S(1)} %get-tuple-element.26.far_weights), custom_call_target="tpu_custom_call" | custom-call | flops 2097152 | bytes 262144 | tf_op jit(solution)/shard_map/pallas_call | solution.py:303
Async XLA Ops:
  0.0 15.7 %copy-start = (bf16[2,4,128,1024]{3,2,1,0:T(8,128)(2,1)S(1)}, bf16[2,4,128,1024]{3,2,1,0:T(8,128)(2,1)}, u32[]{:S(2)}) copy-start(bf16[2,4,128,1024]{3,2,1,0:T(8,128)(2,1)} %near.1) | copy-start | bytes 6291460
  4.1 15.8 %copy-start.2 = (f32[2,16,1024]{2,1,0:T(8,128)S(1)}, f32[2,16,1024]{2,1,0:T(8,128)}, u32[]{:S(2)}) copy-start(f32[2,16,1024]{2,1,0:T(8,128)} %right_side.1) | copy-start | bytes 393220
  4.1 15.8 %copy-start.3 = (bf16[2,32,1024]{2,1,0:T(8,128)(2,1)S(1)}, bf16[2,32,1024]{2,1,0:T(8,128)(2,1)}, u32[]{:S(2)}) copy-start(bf16[2,32,1024]{2,1,0:T(8,128)(2,1)} %basis.1) | copy-start | bytes 393220
  4.1 22.6 %all-to-all-start = ((bf16[128,8,128]{2,1,0:T(8,128)(2,1)}), bf16[128,8,128]{2,1,0:T(8,128)(2,1)S(1)}, u32[]{:S(2)}, u32[]{:S(2)}) async-start(bf16[128,8,128]{2,1,0:T(8,128)(2,1)} %get-tuple-element.16), calls=%async_computation | async-start | bytes 524288 | tf_op jit(solution)/shard_map/all_to_all | solution.py:263
  15.7 4.3 %copy-start.1 = (bf16[2,4,128,1024]{3,2,1,0:T(8,128)(2,1)S(1)}, bf16[2,4,128,1024]{3,2,1,0:T(8,128)(2,1)}, u32[]{:S(2)}) copy-start(bf16[2,4,128,1024]{3,2,1,0:T(8,128)(2,1)} %near_in.1) | copy-start | bytes 6291460
  16.3 7.7 %collective-permute-start = (bf16[16,128]{1,0:T(8,128)(2,1)S(1)}, bf16[16,128]{1,0:T(8,128)(2,1)S(1)}, u32[]{:S(2)}, u32[]{:S(2)}) collective-permute-start(bf16[16,128]{1,0:T(8,128)(2,1)S(1)} %get-tuple-element.19), channel_id=1, source_target_pairs={{0,8},{1,9},{2,10},{3,11},{4,12},{5,13},{6,14},{7,15},{8,0},{9,1},... | collective-permute-start | bytes 12296 | tf_op jit(solution)/shard_map/ppermute | solution.py:191
  17.7 6.4 %collective-permute-start.1 = (bf16[16,128]{1,0:T(8,128)(2,1)S(1)}, bf16[16,128]{1,0:T(8,128)(2,1)S(1)}, u32[]{:S(2)}, u32[]{:S(2)}) collective-permute-start(bf16[16,128]{1,0:T(8,128)(2,1)S(1)} %get-tuple-element.20), channel_id=1, source_target_pairs={{0,1},{1,0},{2,3},{3,2},{4,5},{5,4},{6,7},{7,6},{8,16},{9,17},{10,... | collective-permute-start | bytes 12296 | tf_op jit(solution)/shard_map/ppermute | solution.py:191
  18.4 5.7 %collective-permute-start.2 = (bf16[2,16,128]{2,1,0:T(8,128)(2,1)S(1)}, bf16[2,16,128]{2,1,0:T(8,128)(2,1)S(1)}, u32[]{:S(2)}, u32[]{:S(2)}) collective-permute-start(bf16[2,16,128]{2,1,0:T(8,128)(2,1)S(1)} %get-tuple-element.21), channel_id=1, source_target_pairs={{0,1},{1,0},{2,3},{3,2},{4,5},{5,4},{6,7},{7,6},{8,9},{9,8},{10,11... | collective-permute-start | bytes 24584 | tf_op jit(solution)/shard_map/ppermute | solution.py:191
  18.4 5.7 %collective-permute-start.3 = (bf16[2,16,128]{2,1,0:T(8,128)(2,1)S(1)}, bf16[2,16,128]{2,1,0:T(8,128)(2,1)S(1)}, u32[]{:S(2)}, u32[]{:S(2)}) collective-permute-start(bf16[2,16,128]{2,1,0:T(8,128)(2,1)S(1)} %get-tuple-element.22), channel_id=1, source_target_pairs={{0,7},{1,2},{2,1},{3,4},{4,3},{5,6},{6,5},{7,0},{8,15},{9,10},{10,... | collective-permute-start | bytes 24584 | tf_op jit(solution)/shard_map/ppermute | solution.py:191

commit v4 on v3

--- a/solution.py
+++ b/solution.py
@@ -11,6 +11,7 @@
 HBM = pl.BlockSpec(memory_space=pltpu.HBM)
 MIB = 1024 * 1024
 NT = (((1,), (1,)), ((), ()))
+ALL = ("sec", "y", "core")
 
 
 def iota(shape, dim):
@@ -68,7 +69,8 @@
     second = [
         jnp.broadcast_to(source[:, start : start + lanes], (lanes, lanes)).T > 0.5 for start in range(0, count, lanes)
     ]
-    target = device[...] * 2 + target_half[...].reshape(device.shape)
+    place = device[...] % 2 * (targets // 4) + device[...] // 2
+    target = place * 2 + target_half[...].reshape(device.shape)
     onehot = (iota((targets, count), 0) == target).astype(BF)
 
     sums = None
@@ -91,7 +93,7 @@
 
 
 def even(axis):
-    return lax.rem(lax.axis_index(axis), 2) == 0
+    return lax.axis_index("core") == 0 if axis == "az" else lax.rem(lax.axis_index(axis), 2) == 0
 
 
 def choose(first, yes, no):
@@ -177,7 +179,7 @@
 
 
 def swap(value, axis, start):
-    sec_count, az_count = lax.axis_size("sec"), lax.axis_size("az")
+    sec_count, az_count = lax.axis_size("sec"), 2 * lax.axis_size("y")
     route = []
     for sec in range(sec_count):
         for az in range(az_count):
@@ -188,7 +190,7 @@
                 step = 1 if (sec - start) % 2 == 0 else -1
                 to = (sec + step, az) if 0 <= sec + step < sec_count else (sec, az ^ 1)
             route.append((sec * az_count + az, to[0] * az_count + to[1]))
-    return lax.ppermute(value, ("sec", "az"), route)
+    return lax.ppermute(value, ALL, route)
 
 
 def in_hbm(array):
@@ -230,7 +232,7 @@
     near_rank = near_out.shape[2]
     far_len = far_cores.shape[0]
     sec_count = lax.axis_size("sec")
-    az_count = lax.axis_size("az")
+    az_count = 2 * lax.axis_size("y")
     devices = sec_count * az_count
     width = 256
     chunks = far_cores.shape[1] // width
@@ -260,7 +262,7 @@
             pltpu.SemaphoreType.DMA((6 + steps,)),
         ],
     )(*[in_hbm(x) for x in fetched + [far_cores]])
-    received = lax.all_to_all(packed, ("sec", "az"), split_axis=0, concat_axis=0, tiled=True)
+    received = lax.all_to_all(packed, ("core", "sec", "y"), split_axis=0, concat_axis=0, tiled=True)
 
     sec_a, sec_b, az_a, az_b, kept = call(
         near_out_kernel,
@@ -311,19 +313,7 @@
 
 
 def solution(mesh):
-    in_specs = (
-        P(("sec", "az"), None, None),
-        P(("sec", "az"), None, None),
-        P(("sec", "az")),
-        P(("sec", "az"), None, None),
-        P(("sec", "az"), None, None, None),
-        P(("sec", "az"), None, None, None),
-        P(("sec", "az"), None, None),
-        P(("sec", "az"), None, None),
-        P(("sec", "az"), None),
-        P(("sec", "az"), None),
-        P(("sec", "az")),
-        P(("sec", "az")),
-    )
-    out_specs = P(("sec", "az"), None, None)
-    return jax.shard_map(local, mesh=mesh, in_specs=in_specs, out_specs=out_specs, check_vma=False)
+    sec_count, az_count = mesh.devices.shape
+    inner = jax.sharding.Mesh(mesh.devices.reshape(sec_count, az_count // 2, 2), ALL)
+    in_specs = (P(ALL),) * 12
+    return jax.shard_map(local, mesh=inner, in_specs=in_specs, out_specs=P(ALL), check_vma=False)

time: 28 us -> 27.5 us (0.982)
  waiting for transfers between devices: 2.32 us -> 1.86 us
    all_to_all x1, waiting for transfers between devices: 2.31 us -> 1.85 us  [local(): lax.all_to_all(packed, ('core', 'sec', 'y'), split_axis=0, concat_axis=0,...]
where the time goes in v4:
time: 27.5 us; the launch traced here: 27.4 us
  starting transfers between devices  15.1 us (55%)
  Pallas kernels  10.2 us (37%)
  waiting for transfers between devices  1.86 us (7%)
    all_to_all x1, starting transfers between devices, local(): lax.all_to_all(packed, ('core', 'sec', 'y'), split_axis=0, concat_axis=0,...  11.5 us
    pallas_call x1, Pallas kernels, local(): call(far_out_kernel, (shape((devices, 2 * chunks, lanes)), shape(currents...  4.11 us
    pallas_call x1, Pallas kernels, local(): call(solve_kernel, (shape((2, rhs_count, row_count), F32), shape((2, 3 *...  4.1 us
    ppermute x4, starting transfers between devices, swap(): return lax.ppermute(value, ALL, route)  3.62 us
    all_to_all x1, waiting for transfers between devices, local(): lax.all_to_all(packed, ('core', 'sec', 'y'), split_axis=0, concat_axis=0,...  1.85 us
    pallas_call x1, Pallas kernels, local(): call(far_in_kernel, shape(right_side.shape, F32), [VMEM] * 3, 2 * 2 * rhs...  1.07 us
    pallas_call x1, Pallas kernels, local(): call(near_out_kernel, (piece, piece, pair, pair, pair), [VMEM] * 2, 2 * n...  0.65 us
  transfers between devices with their start and end apart: 5, of which 1 were waited for; matrix products, arithmetic and copies ran while one was open for 0% of the time, Pallas kernels for 18%

profile of v4, /device:TPU:1, one launch (start us, length us, event | category | flops | bytes accessed | tf_op | source)
XLA Modules:
  0.0 27.4 jit_solution(4086984316647103766)
XLA Ops:
  0.0 0.0 copy-start
  0.0 4.1 %shard_map.118 = (bf16[128,8,128]{2,1,0:T(8,128)(2,1)}, bf16[2,16,1024]{2,1,0:T(8,128)(2,1)S(1)}, f32[2,1,1024]{2,1,0:T(1,128)S(1)}) custom-call(s32[2]{0:T(128)} %counts_hbm.1, f32[2,16,1024]{2,1,0:T(8,128)} %currents_hbm.1, bf16[2,32,1024]{2,1,0:T(8,128)(2,1)} %basis_hbm.1, s32[1,1536]{1,0:T(1,128)} %bitcast.1, s32[1536]{0:T(1024)} %target_hbm.1, ...), custom_call_target="tpu_custom_call" | custom-call | flops 805306368 | bytes 3145728 | tf_op jit(solution)/shard_map/pallas_call | solution.py:245
  4.1 0.0 copy-start.2
  4.1 0.0 copy-start.3
  4.1 11.5 %all-to-all-start = ((bf16[128,8,128]{2,1,0:T(8,128)(2,1)}), bf16[128,8,128]{2,1,0:T(8,128)(2,1)S(1)}, u32[]{:S(2)}, u32[]{:S(2)}) async-start(bf16[128,8,128]{2,1,0:T(8,128)(2,1)} %get-tuple-element.16), calls=%async_computation | async-start | bytes 524288 | tf_op jit(solution)/shard_map/all_to_all | solution.py:265
  15.7 0.0 copy-start.1
  15.7 0.0 copy-done
  15.7 0.6 %shard_map.119 = (bf16[16,128]{1,0:T(8,128)(2,1)S(1)}, bf16[16,128]{1,0:T(8,128)(2,1)S(1)}, bf16[2,16,128]{2,1,0:T(8,128)(2,1)S(1)}, bf16[2,16,128]{2,1,0:T(8,128)(2,1)S(1)}, bf16[2,16,128]{2,1,0:T(8,128)(2,1)S(1)}) custom-call(bf16[2,16,1024]{2,1,0:T(8,128)(2,1)S(1)} %get-tuple-element.18.masked, bf16[2,4,128,1024]{3,2,1,0:T(8,128)(2,1)S(1)} %copy-done), custom_call_target="tpu_custom_call" | custom-call | flops 33554432 | bytes 2097152 | tf_op jit(solution)/shard_map/pallas_call | solution.py:267
  16.3 1.4 %collective-permute-start = (bf16[16,128]{1,0:T(8,128)(2,1)S(1)}, bf16[16,128]{1,0:T(8,128)(2,1)S(1)}, u32[]{:S(2)}, u32[]{:S(2)}) collective-permute-start(bf16[16,128]{1,0:T(8,128)(2,1)S(1)} %get-tuple-element.19), channel_id=1, source_target_pairs={{0,8},{1,9},{2,10},{3,11},{4,12},{5,13},{6,14},{7,15},{8,0},{9,1},... | collective-permute-start | bytes 12296 | tf_op jit(solution)/shard_map/ppermute | solution.py:193
  17.7 0.6 %collective-permute-start.1 = (bf16[16,128]{1,0:T(8,128)(2,1)S(1)}, bf16[16,128]{1,0:T(8,128)(2,1)S(1)}, u32[]{:S(2)}, u32[]{:S(2)}) collective-permute-start(bf16[16,128]{1,0:T(8,128)(2,1)S(1)} %get-tuple-element.20), channel_id=1, source_target_pairs={{0,1},{1,0},{2,3},{3,2},{4,5},{5,4},{6,7},{7,6},{8,16},{9,17},{10,... | collective-permute-start | bytes 12296 | tf_op jit(solution)/shard_map/ppermute | solution.py:193
  18.4 0.0 collective-permute-start.2
  18.4 1.6 %collective-permute-start.3 = (bf16[2,16,128]{2,1,0:T(8,128)(2,1)S(1)}, bf16[2,16,128]{2,1,0:T(8,128)(2,1)S(1)}, u32[]{:S(2)}, u32[]{:S(2)}) collective-permute-start(bf16[2,16,128]{2,1,0:T(8,128)(2,1)S(1)} %get-tuple-element.22), channel_id=1, source_target_pairs={{0,7},{1,2},{2,1},{3,4},{4,3},{5,6},{6,5},{7,0},{8,15},{9,10},{10,... | collective-permute-start | bytes 24584 | tf_op jit(solution)/shard_map/ppermute | solution.py:193
  20.0 0.0 copy-done.2
  20.0 0.0 copy-done.3
  20.0 0.0 copy-done.1
  20.0 4.1 %shard_map.120 = (f32[2,16,1024]{2,1,0:T(8,128)S(1)}, bf16[2,384,1024]{2,1,0:T(8,128)(2,1)S(1)}, bf16[64,1024]{1,0:T(8,128)(2,1)S(1)}) custom-call(f32[2,1,1024]{2,1,0:T(1,128)S(1)} %get-tuple-element.17.keep, f32[2,16,1024]{2,1,0:T(8,128)S(1)} %copy-done.2, bf16[2,16,128]{2,1,0:T(8,128)(2,1)S(1)} %get-tuple-element.23.kept, ...), custom_call_target="tpu_custom_call" | custom-call | flops 1879048192 | bytes 4194304 | tf_op jit(solution)/shard_map/pallas_call | solution.py:279
  24.1 0.0 collective-permute-done.sec_a
  24.1 0.0 collective-permute-done.1.sec_b
  24.1 0.0 collective-permute-done.2.az_a
  24.1 0.0 collective-permute-done.3.az_b
  24.1 0.3 %shard_map.121.solved = f32[2,16,1024]{2,1,0:T(8,128)S(1)} custom-call(f32[2,1,1024]{2,1,0:T(1,128)S(1)} %get-tuple-element.17.keep, bf16[16,128]{1,0:T(8,128)(2,1)S(1)} %collective-permute-done.sec_a, bf16[16,128]{1,0:T(8,128)(2,1)S(1)} %collective-permute-done.1.sec_b, bf16[2,16,128]{2,1,0:T(8,128)(2,1)S(1)} %collective-permute-done.2.az_a, ...), custom_call_target="tpu_custom_call" | custom-call | flops 25165824 | bytes 2097152 | tf_op jit(solution)/shard_map/pallas_call | solution.py:296
  24.4 1.9 %all-to-all-done.received = bf16[128,8,128]{2,1,0:T(8,128)(2,1)S(1)} async-done(((bf16[128,8,128]{2,1,0:T(8,128)(2,1)}), bf16[128,8,128]{2,1,0:T(8,128)(2,1)S(1)}, u32[]{:S(2)}, u32[]{:S(2)}) %all-to-all-start) | async-done | bytes 262176 | tf_op jit(solution)/shard_map/all_to_all | solution.py:265
  26.3 1.1 %shard_map.122 = f32[2,16,1024]{2,1,0:T(8,128)} custom-call(bf16[128,8,128]{2,1,0:T(8,128)(2,1)S(1)} %all-to-all-done.received, f32[2,16,1024]{2,1,0:T(8,128)S(1)} %shard_map.121.solved, bf16[64,1024]{1,0:T(8,128)(2,1)S(1)} %get-tuple-element.26.far_weights), custom_call_target="tpu_custom_call" | custom-call | flops 2097152 | bytes 262144 | tf_op jit(solution)/shard_map/pallas_call | solution.py:305
Async XLA Ops:
  0.0 15.7 %copy-start = (bf16[2,4,128,1024]{3,2,1,0:T(8,128)(2,1)S(1)}, bf16[2,4,128,1024]{3,2,1,0:T(8,128)(2,1)}, u32[]{:S(2)}) copy-start(bf16[2,4,128,1024]{3,2,1,0:T(8,128)(2,1)} %near.1) | copy-start | bytes 6291460
  4.1 15.8 %copy-start.2 = (f32[2,16,1024]{2,1,0:T(8,128)S(1)}, f32[2,16,1024]{2,1,0:T(8,128)}, u32[]{:S(2)}) copy-start(f32[2,16,1024]{2,1,0:T(8,128)} %right_side.1) | copy-start | bytes 393220
  4.1 15.8 %copy-start.3 = (bf16[2,32,1024]{2,1,0:T(8,128)(2,1)S(1)}, bf16[2,32,1024]{2,1,0:T(8,128)(2,1)}, u32[]{:S(2)}) copy-start(bf16[2,32,1024]{2,1,0:T(8,128)(2,1)} %basis.1) | copy-start | bytes 393220
  4.1 22.1 %all-to-all-start = ((bf16[128,8,128]{2,1,0:T(8,128)(2,1)}), bf16[128,8,128]{2,1,0:T(8,128)(2,1)S(1)}, u32[]{:S(2)}, u32[]{:S(2)}) async-start(bf16[128,8,128]{2,1,0:T(8,128)(2,1)} %get-tuple-element.16), calls=%async_computation | async-start | bytes 524288 | tf_op jit(solution)/shard_map/all_to_all | solution.py:265
  15.7 4.3 %copy-start.1 = (bf16[2,4,128,1024]{3,2,1,0:T(8,128)(2,1)S(1)}, bf16[2,4,128,1024]{3,2,1,0:T(8,128)(2,1)}, u32[]{:S(2)}) copy-start(bf16[2,4,128,1024]{3,2,1,0:T(8,128)(2,1)} %near_in.1) | copy-start | bytes 6291460
  16.3 7.7 %collective-permute-start = (bf16[16,128]{1,0:T(8,128)(2,1)S(1)}, bf16[16,128]{1,0:T(8,128)(2,1)S(1)}, u32[]{:S(2)}, u32[]{:S(2)}) collective-permute-start(bf16[16,128]{1,0:T(8,128)(2,1)S(1)} %get-tuple-element.19), channel_id=1, source_target_pairs={{0,8},{1,9},{2,10},{3,11},{4,12},{5,13},{6,14},{7,15},{8,0},{9,1},... | collective-permute-start | bytes 12296 | tf_op jit(solution)/shard_map/ppermute | solution.py:193
  17.7 6.4 %collective-permute-start.1 = (bf16[16,128]{1,0:T(8,128)(2,1)S(1)}, bf16[16,128]{1,0:T(8,128)(2,1)S(1)}, u32[]{:S(2)}, u32[]{:S(2)}) collective-permute-start(bf16[16,128]{1,0:T(8,128)(2,1)S(1)} %get-tuple-element.20), channel_id=1, source_target_pairs={{0,1},{1,0},{2,3},{3,2},{4,5},{5,4},{6,7},{7,6},{8,16},{9,17},{10,... | collective-permute-start | bytes 12296 | tf_op jit(solution)/shard_map/ppermute | solution.py:193
  18.4 5.7 %collective-permute-start.2 = (bf16[2,16,128]{2,1,0:T(8,128)(2,1)S(1)}, bf16[2,16,128]{2,1,0:T(8,128)(2,1)S(1)}, u32[]{:S(2)}, u32[]{:S(2)}) collective-permute-start(bf16[2,16,128]{2,1,0:T(8,128)(2,1)S(1)} %get-tuple-element.21), channel_id=1, source_target_pairs={{0,1},{1,0},{2,3},{3,2},{4,5},{5,4},{6,7},{7,6},{8,9},{9,8},{10,11... | collective-permute-start | bytes 24584 | tf_op jit(solution)/shard_map/ppermute | solution.py:193
  18.4 5.7 %collective-permute-start.3 = (bf16[2,16,128]{2,1,0:T(8,128)(2,1)S(1)}, bf16[2,16,128]{2,1,0:T(8,128)(2,1)S(1)}, u32[]{:S(2)}, u32[]{:S(2)}) collective-permute-start(bf16[2,16,128]{2,1,0:T(8,128)(2,1)S(1)} %get-tuple-element.22), channel_id=1, source_target_pairs={{0,7},{1,2},{2,1},{3,4},{4,3},{5,6},{6,5},{7,0},{8,15},{9,10},{10,... | collective-permute-start | bytes 24584 | tf_op jit(solution)/shard_map/ppermute | solution.py:193

commit v5 on v4

--- a/solution.py
+++ b/solution.py
@@ -22,10 +22,10 @@
     return lax.dot_general(a, b, dims, preferred_element_type=F32)
 
 
-def far_out_kernel(
-    counts_hbm, currents_hbm, basis_hbm, device_hbm, target_hbm, source_hbm, cores_hbm,
-    packed, masked, keep,
-    counts, currents, basis, device, target_half, source_half, cores, terms, staged, sems,
+def send_kernel(
+    counts_hbm, currents_hbm, basis_hbm, device_hbm, target_hbm, source_hbm, cores_hbm, near_hbm,
+    packed_hbm, sec_a, sec_b, az_a, az_b, kept, keep,
+    counts, currents, basis, device, target_half, source_half, cores, near, terms, staged, packed, masked, sems,
 ):
     steps, rows = cores.shape[:2]
     pairs = [
@@ -37,6 +37,7 @@
         (source_hbm, source_half),
     ]
     pairs += [(cores_hbm.at[pl.ds(step * rows, rows)], cores.at[step]) for step in range(steps)]
+    pairs += [(near_hbm, near)]
     copies = [pltpu.make_async_copy(source, to, sems.at[i]) for i, (source, to) in enumerate(pairs)]
     for copy in copies:
         copy.start()
@@ -87,20 +88,19 @@
             part = slice((step - 1) * rows, step * rows)
             term = dot(onehot[:, part], terms[part, :])
             sums = term if sums is None else sums + term
-    for k in range(chunks):
-        staged[pl.ds(k, targets, stride=chunks), :] = sums[:, k * lanes : (k + 1) * lanes]
-    packed[...] = staged[...].reshape(packed.shape).astype(BF)
-
-
-def even(axis):
-    return lax.axis_index("core") == 0 if axis == "az" else lax.rem(lax.axis_index(axis), 2) == 0
-
-
-def choose(first, yes, no):
-    return jnp.where(first, yes.astype(F32), no.astype(F32)).astype(BF)
-
-
-def near_out_kernel(masked, near, sec_a, sec_b, az_a, az_b, kept):
+    halves = []
+    for half in range(2):
+        some = targets // 2
+        for k in range(chunks):
+            piece = sums[half * some : (half + 1) * some, k * lanes : (k + 1) * lanes]
+            staged[pl.ds(half * some * chunks + k, some, stride=chunks), :] = piece
+        part = pl.ds(half * some // 2, some // 2)
+        piece = staged[pl.ds(half * some * chunks, some * chunks), :]
+        packed[part] = piece.reshape(some // 2, 2 * chunks, lanes).astype(BF)
+        halves.append(pltpu.make_async_copy(packed.at[part], packed_hbm.at[part], sems.at[7 + steps + half]))
+        halves[-1].start()
+
+    copies[6 + steps].wait()
     rank = sec_a.shape[1]
     sec_even, az_even = even("sec"), even("az")
     coeffs = []
@@ -115,30 +115,46 @@
         to_next, to_previous = coeffs[sub][:, 2 * rank : 3 * rank], coeffs[sub][:, 3 * rank :]
         az_a[sub] = choose(az_even, to_next, to_previous)
         az_b[sub] = choose(az_even, to_previous, to_next)
+    for copy in halves:
+        copy.wait()
+
+
+def even(axis):
+    return lax.axis_index("core") == 0 if axis == "az" else lax.rem(lax.axis_index(axis), 2) == 0
+
+
+def choose(first, yes, no):
+    return jnp.where(first, yes.astype(F32), no.astype(F32)).astype(BF)
 
 
 def solve_kernel(
-    keep, right_side, kept, basis, near_in, inverse_hbm, base, near_weights, far_weights, inverse, sems
+    keep, kept, right_hbm, basis_hbm, near_hbm, inverse_hbm,
+    base, near_weights, far_weights,
+    right_side, basis, near_in, inverse, sems,
 ):
     parts, rows = inverse.shape[1:3]
-    copies = [
-        pltpu.make_async_copy(inverse_hbm.at[sub, pl.ds(part * rows, rows)], inverse.at[sub, part], sems.at[sub, part])
-        for sub in range(2)
-        for part in range(parts)
-    ]
+    pairs = [(right_hbm, right_side), (basis_hbm, basis)]
+    for sub in range(2):
+        pairs.append((near_hbm.at[sub], near_in.at[sub]))
+        pairs += [(inverse_hbm.at[sub, pl.ds(part * rows, rows)], inverse.at[sub, part]) for part in range(parts)]
+    copies = [pltpu.make_async_copy(source, to, sems.at[i]) for i, (source, to) in enumerate(pairs)]
     for copy in copies:
         copy.start()
+    for copy in copies[:2]:
+        copy.wait()
     rhs_count = right_side.shape[1]
     far_rank = basis.shape[1]
     near_rows = near_weights.shape[1]
     for sub in range(2):
+        own = copies[2 + sub * (parts + 1) :]
+        own[0].wait()
         rest = jnp.where(keep[sub] > 0.0, right_side[sub], 0.0) - dot(kept[1 - sub], near_in[sub, 1 - sub])
         high = rest.astype(BF)
         low = (rest - high.astype(F32)).astype(BF)
         factors = [near_in[sub, sub], near_in[sub, 2], near_in[sub, 3]]
         stacked = jnp.concatenate(factors + [high, low, basis[sub]], axis=0)
         for part in range(parts):
-            copies[sub * parts + part].wait()
+            own[1 + part].wait()
             solved = dot(stacked, inverse[sub, part], NT)
             columns = pl.ds(part * rows, rows)
             near_weights[sub, :, columns] = solved[:near_rows].astype(BF)
@@ -197,12 +213,12 @@
     return pltpu.with_memory_space_constraint(array, pltpu.HBM)
 
 
-def call(kernel, out_shape, in_specs, flops, moved, grant, scratch=()):
+def call(kernel, out_shape, in_specs, flops, moved, grant, scratch=(), out_specs=None):
     return pl.pallas_call(
         kernel,
         out_shape=out_shape,
         in_specs=in_specs,
-        out_specs=jax.tree.map(lambda _: VMEM, out_shape),
+        out_specs=out_specs or jax.tree.map(lambda _: VMEM, out_shape),
         scratch_shapes=scratch,
         compiler_params=pltpu.CompilerParams(vmem_limit_bytes=grant * MIB),
         cost_estimate=pl.CostEstimate(flops=flops, bytes_accessed=moved, transcendentals=0),
@@ -242,10 +258,18 @@
     pair = shape((2, rhs_count, near_rank))
     steps = 3
     fetched = [counts, currents, far_source_basis, far_target_device.reshape(1, far_len), far_target_half, far_source_half]
-    packed, masked, keep = call(
-        far_out_kernel,
-        (shape((devices, 2 * chunks, lanes)), shape(currents.shape), shape((2, 1, row_count), F32)),
-        [HBM] * 7,
+    packed, sec_a, sec_b, az_a, az_b, kept, keep = call(
+        send_kernel,
+        (
+            shape((devices, 2 * chunks, lanes)),
+            piece,
+            piece,
+            pair,
+            pair,
+            pair,
+            shape((2, 1, row_count), F32),
+        ),
+        [HBM] * 8,
         2 * 2 * devices * far_len * row_count,
         2 * far_cores.size,
         20,
@@ -257,21 +281,16 @@
             pltpu.VMEM((far_len,), jnp.int32),
             pltpu.VMEM((far_len,), jnp.int32),
             pltpu.VMEM((steps, far_len // steps, far_cores.shape[1]), BF),
+            pltpu.VMEM(near_out.shape, BF),
             pltpu.VMEM((far_len, chunks * lanes), BF),
             pltpu.VMEM((2 * devices * chunks, lanes), F32),
-            pltpu.SemaphoreType.DMA((6 + steps,)),
+            pltpu.VMEM((devices, 2 * chunks, lanes), BF),
+            pltpu.VMEM(currents.shape, BF),
+            pltpu.SemaphoreType.DMA((9 + steps,)),
         ],
-    )(*[in_hbm(x) for x in fetched + [far_cores]])
+        (HBM,) + (VMEM,) * 6,
+    )(*[in_hbm(x) for x in fetched + [far_cores, near_out]])
     received = lax.all_to_all(packed, ("core", "sec", "y"), split_axis=0, concat_axis=0, tiled=True)
-
-    sec_a, sec_b, az_a, az_b, kept = call(
-        near_out_kernel,
-        (piece, piece, pair, pair, pair),
-        [VMEM] * 2,
-        2 * near_out.size * rhs_count,
-        near_out.size * 2,
-        2,
-    )(masked, near_out)
     sec_a, sec_b = swap(sec_a, "sec", 0), swap(sec_b, "sec", 1)
     az_a, az_b = swap(az_a, "az", 0), swap(az_b, "az", 1)
 
@@ -283,15 +302,18 @@
             shape((2, 3 * near_rank, row_count)),
             shape((2 * far_rank, row_count)),
         ),
-        [VMEM] * 5 + [HBM],
+        [VMEM] * 2 + [HBM] * 4,
         2 * inverse_blocks.size * (3 * near_rank + 2 * rhs_count + far_rank),
         inverse_blocks.size * 2,
         16,
         [
+            pltpu.VMEM(right_side.shape, F32),
+            pltpu.VMEM(far_target_basis.shape, BF),
+            pltpu.VMEM(near_in.shape, BF),
             pltpu.VMEM((2, parts, row_count // parts, row_count), BF),
-            pltpu.SemaphoreType.DMA((2, parts)),
+            pltpu.SemaphoreType.DMA((4 + 2 * parts,)),
         ],
-    )(keep, right_side, kept, far_target_basis, near_in, in_hbm(inverse_blocks))
+    )(keep, kept, *[in_hbm(x) for x in [right_side, far_target_basis, near_in, inverse_blocks]])
 
     solved = call(
         near_in_kernel,

time: 27.5 us -> 27.3 us (level)
    pallas_call x2 -> x1, Pallas kernels: 4.75 us -> 3.95 us  [local(): call(send_kernel, (shape((devices, 2 * chunks, lanes)), piece, piece, pai...]
    pallas_call x1, Pallas kernels: 4.1 us -> 4.72 us  [local(): call(solve_kernel, (shape((2, rhs_count, row_count), F32), shape((2, 3 *...]
  transfers between devices with their start and end apart: 5 -> 5, of which waited for: 1 -> 1; matrix products, arithmetic and copies ran while one was open for 0% -> 0% of each run, Pallas kernels for 18% -> 19%
where the time goes in v5:
time: 27.3 us; the launch traced here: 27.2 us
  starting transfers between devices  15.2 us (56%)
  Pallas kernels  10.1 us (37%)
  waiting for transfers between devices  1.86 us (7%)
    all_to_all x1, starting transfers between devices, local(): lax.all_to_all(packed, ('core', 'sec', 'y'), split_axis=0, concat_axis=0,...  11.5 us
    pallas_call x1, Pallas kernels, local(): call(solve_kernel, (shape((2, rhs_count, row_count), F32), shape((2, 3 *...  4.72 us
    pallas_call x1, Pallas kernels, local(): call(send_kernel, (shape((devices, 2 * chunks, lanes)), piece, piece, pai...  3.95 us
    ppermute x4, starting transfers between devices, swap(): return lax.ppermute(value, ALL, route)  3.69 us
    all_to_all x1, waiting for transfers between devices, local(): lax.all_to_all(packed, ('core', 'sec', 'y'), split_axis=0, concat_axis=0,...  1.85 us
    pallas_call x1, Pallas kernels, local(): call(far_in_kernel, shape(right_side.shape, F32), [VMEM] * 3, 2 * 2 * rhs...  1.07 us
  transfers between devices with their start and end apart: 5, of which 1 were waited for; matrix products, arithmetic and copies ran while one was open for 0% of the time, Pallas kernels for 19%

profile of v5, /device:TPU:1, one launch (start us, length us, event | category | flops | bytes accessed | tf_op | source)
XLA Modules:
  0.0 27.2 jit_solution(10929007222282596979)
XLA Ops:
  0.0 4.0 %shard_map.118 = (bf16[128,8,128]{2,1,0:T(8,128)(2,1)}, bf16[16,128]{1,0:T(8,128)(2,1)S(1)}, bf16[16,128]{1,0:T(8,128)(2,1)S(1)}, bf16[2,16,128]{2,1,0:T(8,128)(...) custom-call(s32[2]{0:T(128)} %counts_hbm.1, ...), custom_call_target="tpu_custom_call" | custom-call | flops 805306368 | bytes 3145728 | tf_op jit(solution)/shard_map/pallas_call | solution.py:261
  4.0 11.5 %all-to-all-start = ((bf16[128,8,128]{2,1,0:T(8,128)(2,1)}), bf16[128,8,128]{2,1,0:T(8,128)(2,1)S(1)}, u32[]{:S(2)}, u32[]{:S(2)}) async-start(bf16[128,8,128]{2,1,0:T(8,128)(2,1)} %get-tuple-element.15), calls=%async_computation | async-start | bytes 524288 | tf_op jit(solution)/shard_map/all_to_all | solution.py:293
  15.5 1.5 %collective-permute-start = (bf16[16,128]{1,0:T(8,128)(2,1)S(1)}, bf16[16,128]{1,0:T(8,128)(2,1)S(1)}, u32[]{:S(2)}, u32[]{:S(2)}) collective-permute-start(bf16[16,128]{1,0:T(8,128)(2,1)S(1)} %get-tuple-element.17), channel_id=1, source_target_pairs={{0,8},{1,9},{2,10},{3,11},{4,12},{5,13},{6,14},{7,15},{8,0},{9,1},... | collective-permute-start | bytes 12296 | tf_op jit(solution)/shard_map/ppermute | solution.py:209
  16.9 0.6 %collective-permute-start.1 = (bf16[16,128]{1,0:T(8,128)(2,1)S(1)}, bf16[16,128]{1,0:T(8,128)(2,1)S(1)}, u32[]{:S(2)}, u32[]{:S(2)}) collective-permute-start(bf16[16,128]{1,0:T(8,128)(2,1)S(1)} %get-tuple-element.18), channel_id=1, source_target_pairs={{0,1},{1,0},{2,3},{3,2},{4,5},{5,4},{6,7},{7,6},{8,16},{9,17},{10,... | collective-permute-start | bytes 12296 | tf_op jit(solution)/shard_map/ppermute | solution.py:209
  17.6 0.0 collective-permute-start.2
  17.6 1.6 %collective-permute-start.3 = (bf16[2,16,128]{2,1,0:T(8,128)(2,1)S(1)}, bf16[2,16,128]{2,1,0:T(8,128)(2,1)S(1)}, u32[]{:S(2)}, u32[]{:S(2)}) collective-permute-start(bf16[2,16,128]{2,1,0:T(8,128)(2,1)S(1)} %get-tuple-element.20), channel_id=1, source_target_pairs={{0,7},{1,2},{2,1},{3,4},{4,3},{5,6},{6,5},{7,0},{8,15},{9,10},{10,... | collective-permute-start | bytes 24584 | tf_op jit(solution)/shard_map/ppermute | solution.py:209
  19.2 4.7 %shard_map.119 = (f32[2,16,1024]{2,1,0:T(8,128)S(1)}, bf16[2,384,1024]{2,1,0:T(8,128)(2,1)S(1)}, bf16[64,1024]{1,0:T(8,128)(2,1)S(1)}) custom-call(f32[2,1,1024]{2,1,0:T(1,128)S(1)} %get-tuple-element.16.keep, bf16[2,16,128]{2,1,0:T(8,128)(2,1)S(1)} %get-tuple-element.21.kept, f32[2,16,1024]{2,1,0:T(8,128)} %right_hbm.1, bf16[2,32,1024]{2,1,0:T(8,128)(2,1)} %basis_hbm.3, ...), custom_call_target="tpu_custom_call" | custom-call | flops 1879048192 | bytes 4194304 | tf_op jit(solution)/shard_map/pallas_call | solution.py:298
  23.9 0.0 collective-permute-done.sec_a
  23.9 0.0 collective-permute-done.1.sec_b
  23.9 0.0 collective-permute-done.2.az_a
  23.9 0.0 collective-permute-done.3.az_b
  23.9 0.3 %shard_map.120.solved = f32[2,16,1024]{2,1,0:T(8,128)S(1)} custom-call(f32[2,1,1024]{2,1,0:T(1,128)S(1)} %get-tuple-element.16.keep, bf16[16,128]{1,0:T(8,128)(2,1)S(1)} %collective-permute-done.sec_a, bf16[16,128]{1,0:T(8,128)(2,1)S(1)} %collective-permute-done.1.sec_b, bf16[2,16,128]{2,1,0:T(8,128)(2,1)S(1)} %collective-permute-done.2.az_a, ...), custom_call_target="tpu_custom_call" | custom-call | flops 25165824 | bytes 2097152 | tf_op jit(solution)/shard_map/pallas_call | solution.py:318
  24.2 1.8 %all-to-all-done.received = bf16[128,8,128]{2,1,0:T(8,128)(2,1)S(1)} async-done(((bf16[128,8,128]{2,1,0:T(8,128)(2,1)}), bf16[128,8,128]{2,1,0:T(8,128)(2,1)S(1)}, u32[]{:S(2)}, u32[]{:S(2)}) %all-to-all-start) | async-done | bytes 262176 | tf_op jit(solution)/shard_map/all_to_all | solution.py:293
  26.1 1.1 %shard_map.121 = f32[2,16,1024]{2,1,0:T(8,128)} custom-call(bf16[128,8,128]{2,1,0:T(8,128)(2,1)S(1)} %all-to-all-done.received, f32[2,16,1024]{2,1,0:T(8,128)S(1)} %shard_map.120.solved, bf16[64,1024]{1,0:T(8,128)(2,1)S(1)} %get-tuple-element.24.far_weights), custom_call_target="tpu_custom_call" | custom-call | flops 2097152 | bytes 262144 | tf_op jit(solution)/shard_map/pallas_call | solution.py:327
Async XLA Ops:
  4.0 22.1 %all-to-all-start = ((bf16[128,8,128]{2,1,0:T(8,128)(2,1)}), bf16[128,8,128]{2,1,0:T(8,128)(2,1)S(1)}, u32[]{:S(2)}, u32[]{:S(2)}) async-start(bf16[128,8,128]{2,1,0:T(8,128)(2,1)} %get-tuple-element.15), calls=%async_computation | async-start | bytes 524288 | tf_op jit(solution)/shard_map/all_to_all | solution.py:293
  15.5 8.4 %collective-permute-start = (bf16[16,128]{1,0:T(8,128)(2,1)S(1)}, bf16[16,128]{1,0:T(8,128)(2,1)S(1)}, u32[]{:S(2)}, u32[]{:S(2)}) collective-permute-start(bf16[16,128]{1,0:T(8,128)(2,1)S(1)} %get-tuple-element.17), channel_id=1, source_target_pairs={{0,8},{1,9},{2,10},{3,11},{4,12},{5,13},{6,14},{7,15},{8,0},{9,1},... | collective-permute-start | bytes 12296 | tf_op jit(solution)/shard_map/ppermute | solution.py:209
  16.9 7.0 %collective-permute-start.1 = (bf16[16,128]{1,0:T(8,128)(2,1)S(1)}, bf16[16,128]{1,0:T(8,128)(2,1)S(1)}, u32[]{:S(2)}, u32[]{:S(2)}) collective-permute-start(bf16[16,128]{1,0:T(8,128)(2,1)S(1)} %get-tuple-element.18), channel_id=1, source_target_pairs={{0,1},{1,0},{2,3},{3,2},{4,5},{5,4},{6,7},{7,6},{8,16},{9,17},{10,... | collective-permute-start | bytes 12296 | tf_op jit(solution)/shard_map/ppermute | solution.py:209
  17.6 6.3 %collective-permute-start.2 = (bf16[2,16,128]{2,1,0:T(8,128)(2,1)S(1)}, bf16[2,16,128]{2,1,0:T(8,128)(2,1)S(1)}, u32[]{:S(2)}, u32[]{:S(2)}) collective-permute-start(bf16[2,16,128]{2,1,0:T(8,128)(2,1)S(1)} %get-tuple-element.19), channel_id=1, source_target_pairs={{0,1},{1,0},{2,3},{3,2},{4,5},{5,4},{6,7},{7,6},{8,9},{9,8},{10,11... | collective-permute-start | bytes 24584 | tf_op jit(solution)/shard_map/ppermute | solution.py:209
  17.6 6.3 %collective-permute-start.3 = (bf16[2,16,128]{2,1,0:T(8,128)(2,1)S(1)}, bf16[2,16,128]{2,1,0:T(8,128)(2,1)S(1)}, u32[]{:S(2)}, u32[]{:S(2)}) collective-permute-start(bf16[2,16,128]{2,1,0:T(8,128)(2,1)S(1)} %get-tuple-element.20), channel_id=1, source_target_pairs={{0,7},{1,2},{2,1},{3,4},{4,3},{5,6},{6,5},{7,0},{8,15},{9,10},{10,... | collective-permute-start | bytes 24584 | tf_op jit(solution)/shard_map/ppermute | solution.py:209

commit v6 on v5

--- a/solution.py
+++ b/solution.py
@@ -88,17 +88,11 @@
             part = slice((step - 1) * rows, step * rows)
             term = dot(onehot[:, part], terms[part, :])
             sums = term if sums is None else sums + term
-    halves = []
-    for half in range(2):
-        some = targets // 2
-        for k in range(chunks):
-            piece = sums[half * some : (half + 1) * some, k * lanes : (k + 1) * lanes]
-            staged[pl.ds(half * some * chunks + k, some, stride=chunks), :] = piece
-        part = pl.ds(half * some // 2, some // 2)
-        piece = staged[pl.ds(half * some * chunks, some * chunks), :]
-        packed[part] = piece.reshape(some // 2, 2 * chunks, lanes).astype(BF)
-        halves.append(pltpu.make_async_copy(packed.at[part], packed_hbm.at[part], sems.at[7 + steps + half]))
-        halves[-1].start()
+    for k in range(chunks):
+        staged[pl.ds(k, targets, stride=chunks), :] = sums[:, k * lanes : (k + 1) * lanes]
+    packed[...] = staged[: targets * chunks, :].reshape(packed.shape).astype(BF)
+    sent = pltpu.make_async_copy(packed, packed_hbm, sems.at[7 + steps])
+    sent.start()
 
     copies[6 + steps].wait()
     rank = sec_a.shape[1]
@@ -115,8 +109,7 @@
         to_next, to_previous = coeffs[sub][:, 2 * rank : 3 * rank], coeffs[sub][:, 3 * rank :]
         az_a[sub] = choose(az_even, to_next, to_previous)
         az_b[sub] = choose(az_even, to_previous, to_next)
-    for copy in halves:
-        copy.wait()
+    sent.wait()
 
 
 def even(axis):
@@ -283,10 +276,10 @@
             pltpu.VMEM((steps, far_len // steps, far_cores.shape[1]), BF),
             pltpu.VMEM(near_out.shape, BF),
             pltpu.VMEM((far_len, chunks * lanes), BF),
-            pltpu.VMEM((2 * devices * chunks, lanes), F32),
+            pltpu.VMEM((2 * devices * chunks + 8, lanes), F32),
             pltpu.VMEM((devices, 2 * chunks, lanes), BF),
             pltpu.VMEM(currents.shape, BF),
-            pltpu.SemaphoreType.DMA((9 + steps,)),
+            pltpu.SemaphoreType.DMA((8 + steps,)),
         ],
         (HBM,) + (VMEM,) * 6,
     )(*[in_hbm(x) for x in fetched + [far_cores, near_out]])
@@ -294,7 +287,7 @@
     sec_a, sec_b = swap(sec_a, "sec", 0), swap(sec_b, "sec", 1)
     az_a, az_b = swap(az_a, "az", 0), swap(az_b, "az", 1)
 
-    parts = 2
+    parts = 1
     base, near_weights, far_weights = call(
         solve_kernel,
         (

time: 27.3 us -> 27.3 us (level)
  transfers between devices with their start and end apart: 5 -> 5, of which waited for: 1 -> 1; matrix products, arithmetic and copies ran while one was open for 0% -> 0% of each run, Pallas kernels for 19% -> 18%
where the time goes in v6:
time: 27.3 us; the launch traced here: 27.2 us
  starting transfers between devices  15.2 us (56%)
  Pallas kernels  10 us (37%)
  waiting for transfers between devices  1.9 us (7%)
    all_to_all x1, starting transfers between devices, local(): lax.all_to_all(packed, ('core', 'sec', 'y'), split_axis=0, concat_axis=0,...  11.5 us
    pallas_call x1, Pallas kernels, local(): call(solve_kernel, (shape((2, rhs_count, row_count), F32), shape((2, 3 *...  4.68 us
    pallas_call x1, Pallas kernels, local(): call(send_kernel, (shape((devices, 2 * chunks, lanes)), piece, piece, pai...  3.97 us
    ppermute x4, starting transfers between devices, swap(): return lax.ppermute(value, ALL, route)  3.69 us
    all_to_all x1, waiting for transfers between devices, local(): lax.all_to_all(packed, ('core', 'sec', 'y'), split_axis=0, concat_axis=0,...  1.89 us
    pallas_call x1, Pallas kernels, local(): call(far_in_kernel, shape(right_side.shape, F32), [VMEM] * 3, 2 * 2 * rhs...  1.07 us
  transfers between devices with their start and end apart: 5, of which 1 were waited for; matrix products, arithmetic and copies ran while one was open for 0% of the time, Pallas kernels for 18%

profile of v6, /device:TPU:1, one launch (start us, length us, event | category | flops | bytes accessed | tf_op | source)
XLA Modules:
  0.0 27.2 jit_solution(9164570436448465757)
XLA Ops:
  0.0 4.0 %shard_map.118 = (bf16[128,8,128]{2,1,0:T(8,128)(2,1)}, bf16[16,128]{1,0:T(8,128)(2,1)S(1)}, bf16[16,128]{1,0:T(8,128)(2,1)S(1)}, bf16[2,16,128]{2,1,0:T(8,128)(...) custom-call(s32[2]{0:T(128)} %counts_hbm.1, ...), custom_call_target="tpu_custom_call" | custom-call | flops 805306368 | bytes 3145728 | tf_op jit(solution)/shard_map/pallas_call | solution.py:254
  4.0 11.5 %all-to-all-start = ((bf16[128,8,128]{2,1,0:T(8,128)(2,1)}), bf16[128,8,128]{2,1,0:T(8,128)(2,1)S(1)}, u32[]{:S(2)}, u32[]{:S(2)}) async-start(bf16[128,8,128]{2,1,0:T(8,128)(2,1)} %get-tuple-element.15), calls=%async_computation | async-start | bytes 524288 | tf_op jit(solution)/shard_map/all_to_all | solution.py:286
  15.5 1.5 %collective-permute-start = (bf16[16,128]{1,0:T(8,128)(2,1)S(1)}, bf16[16,128]{1,0:T(8,128)(2,1)S(1)}, u32[]{:S(2)}, u32[]{:S(2)}) collective-permute-start(bf16[16,128]{1,0:T(8,128)(2,1)S(1)} %get-tuple-element.17), channel_id=1, source_target_pairs={{0,8},{1,9},{2,10},{3,11},{4,12},{5,13},{6,14},{7,15},{8,0},{9,1},... | collective-permute-start | bytes 12296 | tf_op jit(solution)/shard_map/ppermute | solution.py:202
  17.0 0.6 %collective-permute-start.1 = (bf16[16,128]{1,0:T(8,128)(2,1)S(1)}, bf16[16,128]{1,0:T(8,128)(2,1)S(1)}, u32[]{:S(2)}, u32[]{:S(2)}) collective-permute-start(bf16[16,128]{1,0:T(8,128)(2,1)S(1)} %get-tuple-element.18), channel_id=1, source_target_pairs={{0,1},{1,0},{2,3},{3,2},{4,5},{5,4},{6,7},{7,6},{8,16},{9,17},{10,... | collective-permute-start | bytes 12296 | tf_op jit(solution)/shard_map/ppermute | solution.py:202
  17.6 0.0 collective-permute-start.2
  17.6 1.6 %collective-permute-start.3 = (bf16[2,16,128]{2,1,0:T(8,128)(2,1)S(1)}, bf16[2,16,128]{2,1,0:T(8,128)(2,1)S(1)}, u32[]{:S(2)}, u32[]{:S(2)}) collective-permute-start(bf16[2,16,128]{2,1,0:T(8,128)(2,1)S(1)} %get-tuple-element.20), channel_id=1, source_target_pairs={{0,7},{1,2},{2,1},{3,4},{4,3},{5,6},{6,5},{7,0},{8,15},{9,10},{10,... | collective-permute-start | bytes 24584 | tf_op jit(solution)/shard_map/ppermute | solution.py:202
  19.2 4.7 %shard_map.119 = (f32[2,16,1024]{2,1,0:T(8,128)S(1)}, bf16[2,384,1024]{2,1,0:T(8,128)(2,1)S(1)}, bf16[64,1024]{1,0:T(8,128)(2,1)S(1)}) custom-call(f32[2,1,1024]{2,1,0:T(1,128)S(1)} %get-tuple-element.16.keep, bf16[2,16,128]{2,1,0:T(8,128)(2,1)S(1)} %get-tuple-element.21.kept, f32[2,16,1024]{2,1,0:T(8,128)} %right_hbm.1, bf16[2,32,1024]{2,1,0:T(8,128)(2,1)} %basis_hbm.3, ...), custom_call_target="tpu_custom_call" | custom-call | flops 1879048192 | bytes 4194304 | tf_op jit(solution)/shard_map/pallas_call | solution.py:291
  23.9 0.0 collective-permute-done.sec_a
  23.9 0.0 collective-permute-done.1.sec_b
  23.9 0.0 collective-permute-done.2.az_a
  23.9 0.0 collective-permute-done.3.az_b
  23.9 0.3 %shard_map.120.solved = f32[2,16,1024]{2,1,0:T(8,128)S(1)} custom-call(f32[2,1,1024]{2,1,0:T(1,128)S(1)} %get-tuple-element.16.keep, bf16[16,128]{1,0:T(8,128)(2,1)S(1)} %collective-permute-done.sec_a, bf16[16,128]{1,0:T(8,128)(2,1)S(1)} %collective-permute-done.1.sec_b, bf16[2,16,128]{2,1,0:T(8,128)(2,1)S(1)} %collective-permute-done.2.az_a, ...), custom_call_target="tpu_custom_call" | custom-call | flops 25165824 | bytes 2097152 | tf_op jit(solution)/shard_map/pallas_call | solution.py:311
  24.2 1.9 %all-to-all-done.received = bf16[128,8,128]{2,1,0:T(8,128)(2,1)S(1)} async-done(((bf16[128,8,128]{2,1,0:T(8,128)(2,1)}), bf16[128,8,128]{2,1,0:T(8,128)(2,1)S(1)}, u32[]{:S(2)}, u32[]{:S(2)}) %all-to-all-start) | async-done | bytes 262176 | tf_op jit(solution)/shard_map/all_to_all | solution.py:286
  26.1 1.1 %shard_map.121 = f32[2,16,1024]{2,1,0:T(8,128)} custom-call(bf16[128,8,128]{2,1,0:T(8,128)(2,1)S(1)} %all-to-all-done.received, f32[2,16,1024]{2,1,0:T(8,128)S(1)} %shard_map.120.solved, bf16[64,1024]{1,0:T(8,128)(2,1)S(1)} %get-tuple-element.24.far_weights), custom_call_target="tpu_custom_call" | custom-call | flops 2097152 | bytes 262144 | tf_op jit(solution)/shard_map/pallas_call | solution.py:320
Async XLA Ops:
  4.0 22.1 %all-to-all-start = ((bf16[128,8,128]{2,1,0:T(8,128)(2,1)}), bf16[128,8,128]{2,1,0:T(8,128)(2,1)S(1)}, u32[]{:S(2)}, u32[]{:S(2)}) async-start(bf16[128,8,128]{2,1,0:T(8,128)(2,1)} %get-tuple-element.15), calls=%async_computation | async-start | bytes 524288 | tf_op jit(solution)/shard_map/all_to_all | solution.py:286
  15.5 8.4 %collective-permute-start = (bf16[16,128]{1,0:T(8,128)(2,1)S(1)}, bf16[16,128]{1,0:T(8,128)(2,1)S(1)}, u32[]{:S(2)}, u32[]{:S(2)}) collective-permute-start(bf16[16,128]{1,0:T(8,128)(2,1)S(1)} %get-tuple-element.17), channel_id=1, source_target_pairs={{0,8},{1,9},{2,10},{3,11},{4,12},{5,13},{6,14},{7,15},{8,0},{9,1},... | collective-permute-start | bytes 12296 | tf_op jit(solution)/shard_map/ppermute | solution.py:202
  17.0 6.9 %collective-permute-start.1 = (bf16[16,128]{1,0:T(8,128)(2,1)S(1)}, bf16[16,128]{1,0:T(8,128)(2,1)S(1)}, u32[]{:S(2)}, u32[]{:S(2)}) collective-permute-start(bf16[16,128]{1,0:T(8,128)(2,1)S(1)} %get-tuple-element.18), channel_id=1, source_target_pairs={{0,1},{1,0},{2,3},{3,2},{4,5},{5,4},{6,7},{7,6},{8,16},{9,17},{10,... | collective-permute-start | bytes 12296 | tf_op jit(solution)/shard_map/ppermute | solution.py:202
  17.6 6.3 %collective-permute-start.2 = (bf16[2,16,128]{2,1,0:T(8,128)(2,1)S(1)}, bf16[2,16,128]{2,1,0:T(8,128)(2,1)S(1)}, u32[]{:S(2)}, u32[]{:S(2)}) collective-permute-start(bf16[2,16,128]{2,1,0:T(8,128)(2,1)S(1)} %get-tuple-element.19), channel_id=1, source_target_pairs={{0,1},{1,0},{2,3},{3,2},{4,5},{5,4},{6,7},{7,6},{8,9},{9,8},{10,11... | collective-permute-start | bytes 24584 | tf_op jit(solution)/shard_map/ppermute | solution.py:202
  17.6 6.3 %collective-permute-start.3 = (bf16[2,16,128]{2,1,0:T(8,128)(2,1)S(1)}, bf16[2,16,128]{2,1,0:T(8,128)(2,1)S(1)}, u32[]{:S(2)}, u32[]{:S(2)}) collective-permute-start(bf16[2,16,128]{2,1,0:T(8,128)(2,1)S(1)} %get-tuple-element.20), channel_id=1, source_target_pairs={{0,7},{1,2},{2,1},{3,4},{4,3},{5,6},{6,5},{7,0},{8,15},{9,10},{10,... | collective-permute-start | bytes 24584 | tf_op jit(solution)/shard_map/ppermute | solution.py:202

commit v7 on v6

--- a/solution.py
+++ b/solution.py
@@ -54,16 +54,15 @@
     for sub in range(2):
         keep[sub] = (iota(keep.shape[1:], 1) < counts[sub]).astype(F32)
         masked[sub] = jnp.where(iota(currents.shape[1:], 1) < counts[sub], currents[sub], 0.0).astype(BF)
-    both_masked = jnp.concatenate([masked[0], masked[1]], axis=0)
-    projected = [dot(basis[sub], both_masked, NT).astype(BF) for sub in range(2)]
-    size = (2 * rhs_count, 2 * lanes)
-    repeat = iota(size, 1) // lanes * rhs_count + iota(size, 1) % rhs_count == iota(size, 0)
-    repeat = repeat.astype(BF)
-    size = (width, 2 * lanes)
-    diagonal = iota(size, 0) // far_rank == iota(size, 1) % lanes // rhs_count
-    tiled = [dot(projected[sub], repeat)[:, sub * lanes : (sub + 1) * lanes] for sub in range(2)]
-    tiled = jnp.concatenate([jnp.concatenate(tiled, axis=1)] * (width // far_rank), axis=0)
-    spread = jnp.where(diagonal, tiled, 0.0).astype(BF)
+    copied = lanes // rhs_count
+    size = (width, lanes)
+    diagonal = iota(size, 0) // far_rank == iota(size, 1) // rhs_count
+    spread = []
+    for sub in range(2):
+        projected = dot(basis[sub], jnp.concatenate([masked[sub]] * copied, axis=0), NT)
+        tiled = jnp.concatenate([projected] * (width // far_rank), axis=0)
+        spread.append(jnp.where(diagonal, tiled, 0.0).astype(BF))
+    spread = jnp.concatenate(spread, axis=1)
 
     source = source_half[...].reshape(device.shape).astype(F32)
     count = device.shape[1]

time: 27.3 us -> 27.4 us (level)
  no operation moved by 1% of the time
where the time goes in v7:
time: 27.4 us; the launch traced here: 27.2 us
  starting transfers between devices  15.2 us (55%)
  Pallas kernels  10.1 us (37%)
  waiting for transfers between devices  1.9 us (7%)
    all_to_all x1, starting transfers between devices, local(): lax.all_to_all(packed, ('core', 'sec', 'y'), split_axis=0, concat_axis=0,...  11.5 us
    pallas_call x1, Pallas kernels, local(): call(solve_kernel, (shape((2, rhs_count, row_count), F32), shape((2, 3 *...  4.68 us
    pallas_call x1, Pallas kernels, local(): call(send_kernel, (shape((devices, 2 * chunks, lanes)), piece, piece, pai...  4.02 us
    ppermute x4, starting transfers between devices, swap(): return lax.ppermute(value, ALL, route)  3.69 us
    all_to_all x1, waiting for transfers between devices, local(): lax.all_to_all(packed, ('core', 'sec', 'y'), split_axis=0, concat_axis=0,...  1.89 us
    pallas_call x1, Pallas kernels, local(): call(far_in_kernel, shape(right_side.shape, F32), [VMEM] * 3, 2 * 2 * rhs...  1.07 us
  transfers between devices with their start and end apart: 5, of which 1 were waited for; matrix products, arithmetic and copies ran while one was open for 0% of the time, Pallas kernels for 18%

profile of v7, /device:TPU:1, one launch (start us, length us, event | category | flops | bytes accessed | tf_op | source)
XLA Modules:
  0.0 27.2 jit_solution(18415288102273562546)
XLA Ops:
  0.0 4.0 %shard_map.118 = (bf16[128,8,128]{2,1,0:T(8,128)(2,1)}, bf16[16,128]{1,0:T(8,128)(2,1)S(1)}, bf16[16,128]{1,0:T(8,128)(2,1)S(1)}, bf16[2,16,128]{2,1,0:T(8,128)(...) custom-call(s32[2]{0:T(128)} %counts_hbm.1, ...), custom_call_target="tpu_custom_call" | custom-call | flops 805306368 | bytes 3145728 | tf_op jit(solution)/shard_map/pallas_call | solution.py:253
  4.0 11.5 %all-to-all-start = ((bf16[128,8,128]{2,1,0:T(8,128)(2,1)}), bf16[128,8,128]{2,1,0:T(8,128)(2,1)S(1)}, u32[]{:S(2)}, u32[]{:S(2)}) async-start(bf16[128,8,128]{2,1,0:T(8,128)(2,1)} %get-tuple-element.15), calls=%async_computation | async-start | bytes 524288 | tf_op jit(solution)/shard_map/all_to_all | solution.py:285
  15.5 1.5 %collective-permute-start = (bf16[16,128]{1,0:T(8,128)(2,1)S(1)}, bf16[16,128]{1,0:T(8,128)(2,1)S(1)}, u32[]{:S(2)}, u32[]{:S(2)}) collective-permute-start(bf16[16,128]{1,0:T(8,128)(2,1)S(1)} %get-tuple-element.17), channel_id=1, source_target_pairs={{0,8},{1,9},{2,10},{3,11},{4,12},{5,13},{6,14},{7,15},{8,0},{9,1},... | collective-permute-start | bytes 12296 | tf_op jit(solution)/shard_map/ppermute | solution.py:201
  17.0 0.6 %collective-permute-start.1 = (bf16[16,128]{1,0:T(8,128)(2,1)S(1)}, bf16[16,128]{1,0:T(8,128)(2,1)S(1)}, u32[]{:S(2)}, u32[]{:S(2)}) collective-permute-start(bf16[16,128]{1,0:T(8,128)(2,1)S(1)} %get-tuple-element.18), channel_id=1, source_target_pairs={{0,1},{1,0},{2,3},{3,2},{4,5},{5,4},{6,7},{7,6},{8,16},{9,17},{10,... | collective-permute-start | bytes 12296 | tf_op jit(solution)/shard_map/ppermute | solution.py:201
  17.6 0.0 collective-permute-start.2
  17.6 1.6 %collective-permute-start.3 = (bf16[2,16,128]{2,1,0:T(8,128)(2,1)S(1)}, bf16[2,16,128]{2,1,0:T(8,128)(2,1)S(1)}, u32[]{:S(2)}, u32[]{:S(2)}) collective-permute-start(bf16[2,16,128]{2,1,0:T(8,128)(2,1)S(1)} %get-tuple-element.20), channel_id=1, source_target_pairs={{0,7},{1,2},{2,1},{3,4},{4,3},{5,6},{6,5},{7,0},{8,15},{9,10},{10,... | collective-permute-start | bytes 24584 | tf_op jit(solution)/shard_map/ppermute | solution.py:201
  19.2 4.7 %shard_map.119 = (f32[2,16,1024]{2,1,0:T(8,128)S(1)}, bf16[2,384,1024]{2,1,0:T(8,128)(2,1)S(1)}, bf16[64,1024]{1,0:T(8,128)(2,1)S(1)}) custom-call(f32[2,1,1024]{2,1,0:T(1,128)S(1)} %get-tuple-element.16.keep, bf16[2,16,128]{2,1,0:T(8,128)(2,1)S(1)} %get-tuple-element.21.kept, f32[2,16,1024]{2,1,0:T(8,128)} %right_hbm.1, bf16[2,32,1024]{2,1,0:T(8,128)(2,1)} %basis_hbm.3, ...), custom_call_target="tpu_custom_call" | custom-call | flops 1879048192 | bytes 4194304 | tf_op jit(solution)/shard_map/pallas_call | solution.py:290
  23.9 0.0 collective-permute-done.sec_a
  23.9 0.0 collective-permute-done.1.sec_b
  23.9 0.0 collective-permute-done.2.az_a
  23.9 0.0 collective-permute-done.3.az_b
  24.0 0.3 %shard_map.120.solved = f32[2,16,1024]{2,1,0:T(8,128)S(1)} custom-call(f32[2,1,1024]{2,1,0:T(1,128)S(1)} %get-tuple-element.16.keep, bf16[16,128]{1,0:T(8,128)(2,1)S(1)} %collective-permute-done.sec_a, bf16[16,128]{1,0:T(8,128)(2,1)S(1)} %collective-permute-done.1.sec_b, bf16[2,16,128]{2,1,0:T(8,128)(2,1)S(1)} %collective-permute-done.2.az_a, ...), custom_call_target="tpu_custom_call" | custom-call | flops 25165824 | bytes 2097152 | tf_op jit(solution)/shard_map/pallas_call | solution.py:310
  24.3 1.9 %all-to-all-done.received = bf16[128,8,128]{2,1,0:T(8,128)(2,1)S(1)} async-done(((bf16[128,8,128]{2,1,0:T(8,128)(2,1)}), bf16[128,8,128]{2,1,0:T(8,128)(2,1)S(1)}, u32[]{:S(2)}, u32[]{:S(2)}) %all-to-all-start) | async-done | bytes 262176 | tf_op jit(solution)/shard_map/all_to_all | solution.py:285
  26.2 1.1 %shard_map.121 = f32[2,16,1024]{2,1,0:T(8,128)} custom-call(bf16[128,8,128]{2,1,0:T(8,128)(2,1)S(1)} %all-to-all-done.received, f32[2,16,1024]{2,1,0:T(8,128)S(1)} %shard_map.120.solved, bf16[64,1024]{1,0:T(8,128)(2,1)S(1)} %get-tuple-element.24.far_weights), custom_call_target="tpu_custom_call" | custom-call | flops 2097152 | bytes 262144 | tf_op jit(solution)/shard_map/pallas_call | solution.py:319
Async XLA Ops:
  4.0 22.1 %all-to-all-start = ((bf16[128,8,128]{2,1,0:T(8,128)(2,1)}), bf16[128,8,128]{2,1,0:T(8,128)(2,1)S(1)}, u32[]{:S(2)}, u32[]{:S(2)}) async-start(bf16[128,8,128]{2,1,0:T(8,128)(2,1)} %get-tuple-element.15), calls=%async_computation | async-start | bytes 524288 | tf_op jit(solution)/shard_map/all_to_all | solution.py:285
  15.5 8.4 %collective-permute-start = (bf16[16,128]{1,0:T(8,128)(2,1)S(1)}, bf16[16,128]{1,0:T(8,128)(2,1)S(1)}, u32[]{:S(2)}, u32[]{:S(2)}) collective-permute-start(bf16[16,128]{1,0:T(8,128)(2,1)S(1)} %get-tuple-element.17), channel_id=1, source_target_pairs={{0,8},{1,9},{2,10},{3,11},{4,12},{5,13},{6,14},{7,15},{8,0},{9,1},... | collective-permute-start | bytes 12296 | tf_op jit(solution)/shard_map/ppermute | solution.py:201
  17.0 6.9 %collective-permute-start.1 = (bf16[16,128]{1,0:T(8,128)(2,1)S(1)}, bf16[16,128]{1,0:T(8,128)(2,1)S(1)}, u32[]{:S(2)}, u32[]{:S(2)}) collective-permute-start(bf16[16,128]{1,0:T(8,128)(2,1)S(1)} %get-tuple-element.18), channel_id=1, source_target_pairs={{0,1},{1,0},{2,3},{3,2},{4,5},{5,4},{6,7},{7,6},{8,16},{9,17},{10,... | collective-permute-start | bytes 12296 | tf_op jit(solution)/shard_map/ppermute | solution.py:201
  17.6 6.3 %collective-permute-start.2 = (bf16[2,16,128]{2,1,0:T(8,128)(2,1)S(1)}, bf16[2,16,128]{2,1,0:T(8,128)(2,1)S(1)}, u32[]{:S(2)}, u32[]{:S(2)}) collective-permute-start(bf16[2,16,128]{2,1,0:T(8,128)(2,1)S(1)} %get-tuple-element.19), channel_id=1, source_target_pairs={{0,1},{1,0},{2,3},{3,2},{4,5},{5,4},{6,7},{7,6},{8,9},{9,8},{10,11... | collective-permute-start | bytes 24584 | tf_op jit(solution)/shard_map/ppermute | solution.py:201
  17.6 6.3 %collective-permute-start.3 = (bf16[2,16,128]{2,1,0:T(8,128)(2,1)S(1)}, bf16[2,16,128]{2,1,0:T(8,128)(2,1)S(1)}, u32[]{:S(2)}, u32[]{:S(2)}) collective-permute-start(bf16[2,16,128]{2,1,0:T(8,128)(2,1)S(1)} %get-tuple-element.20), channel_id=1, source_target_pairs={{0,7},{1,2},{2,1},{3,4},{4,3},{5,6},{6,5},{7,0},{8,15},{9,10},{10,... | collective-permute-start | bytes 24584 | tf_op jit(solution)/shard_map/ppermute | solution.py:201

commit v8 on v6

--- a/solution.py
+++ b/solution.py
@@ -157,7 +157,11 @@
             far_weights[pl.ds(sub * far_rank, far_rank), columns] = rest.astype(BF)
 
 
-def near_in_kernel(keep, sec_a, sec_b, az_a, az_b, base, near_weights, solved):
+def near_in_kernel(keep, sec_a, sec_b, az_a, az_b, base, near_weights, solved, select, block):
+    rhs_count = base.shape[1]
+    rank = select.shape[1] // 2
+    select[...] = (iota(select.shape, 0) // rhs_count == iota(select.shape, 1) % rank).astype(BF)
+    block[...] = (iota(block.shape, 0) // rhs_count == iota(block.shape, 1) // rank).astype(F32)
     sec_even, az_even = even("sec"), even("az")
     section = lax.axis_index("sec")
     above = jnp.where(section == 0, 0.0, choose(sec_even, sec_b[...], sec_a[...]).astype(F32))
@@ -169,20 +173,16 @@
         solved[sub] = jnp.where(keep[sub] > 0.0, base[sub] - near_term, 0.0)
 
 
-def far_in_kernel(received, solved, far_weights, out):
+def far_in_kernel(received, solved, far_weights, select, block, out):
     rhs_count = solved.shape[1]
-    rank = far_weights.shape[0] // 2
     sums = jnp.sum(received[...].astype(F32), axis=0)
     chunks = sums.shape[0] // 2
     lanes = sums.shape[1]
     own = iota((rhs_count, lanes), 1) % rhs_count == iota((rhs_count, lanes), 0)
     spaced = [jnp.where(own, sums[row : row + 1], 0.0).astype(BF) for row in range(2 * chunks)]
     spaced = [jnp.concatenate(spaced[sub * chunks : (sub + 1) * chunks], axis=1) for sub in range(2)]
-    size = (chunks * lanes, 2 * rank)
-    select = (iota(size, 0) // rhs_count == iota(size, 1) % rank).astype(BF)
-    far_in = dot(jnp.concatenate(spaced, axis=0), select)
-    block = iota(far_in.shape, 0) // rhs_count == iota(far_in.shape, 1) // rank
-    far_term = dot(jnp.where(block, far_in, 0.0).astype(BF), far_weights[...])
+    far_in = dot(jnp.concatenate(spaced, axis=0), select[...])
+    far_term = dot((far_in * block[...]).astype(BF), far_weights[...])
     for sub in range(2):
         out[sub] = solved[sub] - far_term[sub * rhs_count : (sub + 1) * rhs_count]
 
@@ -308,9 +308,13 @@
         ],
     )(keep, kept, *[in_hbm(x) for x in [right_side, far_target_basis, near_in, inverse_blocks]])
 
-    solved = call(
+    solved, select, block = call(
         near_in_kernel,
-        shape(right_side.shape, F32),
+        (
+            shape(right_side.shape, F32),
+            shape((chunks * lanes, 2 * far_rank)),
+            shape((2 * rhs_count, 2 * far_rank), F32),
+        ),
         [VMEM] * 7,
         2 * 2 * rhs_count * 3 * near_rank * row_count,
         2 * near_in.size,
@@ -320,11 +324,11 @@
     return call(
         far_in_kernel,
         shape(right_side.shape, F32),
-        [VMEM] * 3,
+        [VMEM] * 5,
         2 * 2 * rhs_count * far_rank * row_count,
         received.size * 2,
         4,
-    )(received, solved, far_weights)
+    )(received, solved, far_weights, select, block)
 
 
 def solution(mesh):

time: 27.3 us -> 27.3 us (level)
  transfers between devices with their start and end apart: 5 -> 5, of which waited for: 1 -> 1; matrix products, arithmetic and copies ran while one was open for 0% -> 0% of each run, Pallas kernels for 18% -> 19%
where the time goes in v8:
time: 27.3 us; the launch traced here: 27.2 us
  starting transfers between devices  15.2 us (56%)
  Pallas kernels  10.1 us (37%)
  waiting for transfers between devices  1.85 us (7%)
    all_to_all x1, starting transfers between devices, local(): lax.all_to_all(packed, ('core', 'sec', 'y'), split_axis=0, concat_axis=0,...  11.5 us
    pallas_call x1, Pallas kernels, local(): call(solve_kernel, (shape((2, rhs_count, row_count), F32), shape((2, 3 *...  4.68 us
    pallas_call x1, Pallas kernels, local(): call(send_kernel, (shape((devices, 2 * chunks, lanes)), piece, piece, pai...  3.96 us
    ppermute x4, starting transfers between devices, swap(): return lax.ppermute(value, ALL, route)  3.69 us
    all_to_all x1, waiting for transfers between devices, local(): lax.all_to_all(packed, ('core', 'sec', 'y'), split_axis=0, concat_axis=0,...  1.84 us
    pallas_call x1, Pallas kernels, local(): call(far_in_kernel, shape(right_side.shape, F32), [VMEM] * 5, 2 * 2 * rhs...  1.06 us
  transfers between devices with their start and end apart: 5, of which 1 were waited for; matrix products, arithmetic and copies ran while one was open for 0% of the time, Pallas kernels for 19%

profile of v8, /device:TPU:1, one launch (start us, length us, event | category | flops | bytes accessed | tf_op | source)
XLA Modules:
  0.0 27.2 jit_solution(6776481809200906998)
XLA Ops:
  0.0 4.0 %shard_map.118 = (bf16[128,8,128]{2,1,0:T(8,128)(2,1)}, bf16[16,128]{1,0:T(8,128)(2,1)S(1)}, bf16[16,128]{1,0:T(8,128)(2,1)S(1)}, bf16[2,16,128]{2,1,0:T(8,128)(...) custom-call(s32[2]{0:T(128)} %counts_hbm.1, ...), custom_call_target="tpu_custom_call" | custom-call | flops 805306368 | bytes 3145728 | tf_op jit(solution)/shard_map/pallas_call | solution.py:254
  4.0 11.5 %all-to-all-start = ((bf16[128,8,128]{2,1,0:T(8,128)(2,1)}), bf16[128,8,128]{2,1,0:T(8,128)(2,1)S(1)}, u32[]{:S(2)}, u32[]{:S(2)}) async-start(bf16[128,8,128]{2,1,0:T(8,128)(2,1)} %get-tuple-element.18), calls=%async_computation | async-start | bytes 524288 | tf_op jit(solution)/shard_map/all_to_all | solution.py:286
  15.5 1.5 %collective-permute-start = (bf16[16,128]{1,0:T(8,128)(2,1)S(1)}, bf16[16,128]{1,0:T(8,128)(2,1)S(1)}, u32[]{:S(2)}, u32[]{:S(2)}) collective-permute-start(bf16[16,128]{1,0:T(8,128)(2,1)S(1)} %get-tuple-element.20), channel_id=1, source_target_pairs={{0,8},{1,9},{2,10},{3,11},{4,12},{5,13},{6,14},{7,15},{8,0},{9,1},... | collective-permute-start | bytes 12296 | tf_op jit(solution)/shard_map/ppermute | solution.py:202
  16.9 0.6 %collective-permute-start.1 = (bf16[16,128]{1,0:T(8,128)(2,1)S(1)}, bf16[16,128]{1,0:T(8,128)(2,1)S(1)}, u32[]{:S(2)}, u32[]{:S(2)}) collective-permute-start(bf16[16,128]{1,0:T(8,128)(2,1)S(1)} %get-tuple-element.21), channel_id=1, source_target_pairs={{0,1},{1,0},{2,3},{3,2},{4,5},{5,4},{6,7},{7,6},{8,16},{9,17},{10,... | collective-permute-start | bytes 12296 | tf_op jit(solution)/shard_map/ppermute | solution.py:202
  17.6 0.0 collective-permute-start.2
  17.6 1.6 %collective-permute-start.3 = (bf16[2,16,128]{2,1,0:T(8,128)(2,1)S(1)}, bf16[2,16,128]{2,1,0:T(8,128)(2,1)S(1)}, u32[]{:S(2)}, u32[]{:S(2)}) collective-permute-start(bf16[2,16,128]{2,1,0:T(8,128)(2,1)S(1)} %get-tuple-element.23), channel_id=1, source_target_pairs={{0,7},{1,2},{2,1},{3,4},{4,3},{5,6},{6,5},{7,0},{8,15},{9,10},{10,... | collective-permute-start | bytes 24584 | tf_op jit(solution)/shard_map/ppermute | solution.py:202
  19.2 4.7 %shard_map.119 = (f32[2,16,1024]{2,1,0:T(8,128)S(1)}, bf16[2,384,1024]{2,1,0:T(8,128)(2,1)S(1)}, bf16[64,1024]{1,0:T(8,128)(2,1)S(1)}) custom-call(f32[2,1,1024]{2,1,0:T(1,128)S(1)} %get-tuple-element.19.keep, bf16[2,16,128]{2,1,0:T(8,128)(2,1)S(1)} %get-tuple-element.24.kept, f32[2,16,1024]{2,1,0:T(8,128)} %right_hbm.1, bf16[2,32,1024]{2,1,0:T(8,128)(2,1)} %basis_hbm.3, ...), custom_call_target="tpu_custom_call" | custom-call | flops 1879048192 | bytes 4194304 | tf_op jit(solution)/shard_map/pallas_call | solution.py:291
  23.9 0.0 collective-permute-done.sec_a
  23.9 0.0 collective-permute-done.1.sec_b
  23.9 0.0 collective-permute-done.2.az_a
  23.9 0.0 collective-permute-done.3.az_b
  23.9 0.4 %shard_map.120 = (f32[2,16,1024]{2,1,0:T(8,128)S(1)}, bf16[512,64]{1,0:T(8,128)(2,1)S(1)}, f32[32,64]{1,0:T(8,128)S(1)}) custom-call(f32[2,1,1024]{2,1,0:T(1,128)S(1)} %get-tuple-element.19.keep, bf16[16,128]{1,0:T(8,128)(2,1)S(1)} %collective-permute-done.sec_a, bf16[16,128]{1,0:T(8,128)(2,1)S(1)} %collective-permute-done.1.sec_b, ...), custom_call_target="tpu_custom_call" | custom-call | flops 25165824 | bytes 2097152 | tf_op jit(solution)/shard_map/pallas_call | solution.py:311
  24.3 1.8 %all-to-all-done.received = bf16[128,8,128]{2,1,0:T(8,128)(2,1)S(1)} async-done(((bf16[128,8,128]{2,1,0:T(8,128)(2,1)}), bf16[128,8,128]{2,1,0:T(8,128)(2,1)S(1)}, u32[]{:S(2)}, u32[]{:S(2)}) %all-to-all-start) | async-done | bytes 262176 | tf_op jit(solution)/shard_map/all_to_all | solution.py:286
  26.1 1.1 %shard_map.121 = f32[2,16,1024]{2,1,0:T(8,128)} custom-call(bf16[128,8,128]{2,1,0:T(8,128)(2,1)S(1)} %all-to-all-done.received, f32[2,16,1024]{2,1,0:T(8,128)S(1)} %get-tuple-element.27.solved, bf16[64,1024]{1,0:T(8,128)(2,1)S(1)} %get-tuple-element.28.far_weights, bf16[512,64]{1,0:T(8,128)(2,1)S(1)} %get-tuple-element.29.select, ...), custom_call_target="tpu_custom_call" | custom-call | flops 2097152 | bytes 262144 | tf_op jit(solution)/shard_map/pallas_call | solution.py:324
Async XLA Ops:
  4.0 22.1 %all-to-all-start = ((bf16[128,8,128]{2,1,0:T(8,128)(2,1)}), bf16[128,8,128]{2,1,0:T(8,128)(2,1)S(1)}, u32[]{:S(2)}, u32[]{:S(2)}) async-start(bf16[128,8,128]{2,1,0:T(8,128)(2,1)} %get-tuple-element.18), calls=%async_computation | async-start | bytes 524288 | tf_op jit(solution)/shard_map/all_to_all | solution.py:286
  15.5 8.4 %collective-permute-start = (bf16[16,128]{1,0:T(8,128)(2,1)S(1)}, bf16[16,128]{1,0:T(8,128)(2,1)S(1)}, u32[]{:S(2)}, u32[]{:S(2)}) collective-permute-start(bf16[16,128]{1,0:T(8,128)(2,1)S(1)} %get-tuple-element.20), channel_id=1, source_target_pairs={{0,8},{1,9},{2,10},{3,11},{4,12},{5,13},{6,14},{7,15},{8,0},{9,1},... | collective-permute-start | bytes 12296 | tf_op jit(solution)/shard_map/ppermute | solution.py:202
  16.9 6.9 %collective-permute-start.1 = (bf16[16,128]{1,0:T(8,128)(2,1)S(1)}, bf16[16,128]{1,0:T(8,128)(2,1)S(1)}, u32[]{:S(2)}, u32[]{:S(2)}) collective-permute-start(bf16[16,128]{1,0:T(8,128)(2,1)S(1)} %get-tuple-element.21), channel_id=1, source_target_pairs={{0,1},{1,0},{2,3},{3,2},{4,5},{5,4},{6,7},{7,6},{8,16},{9,17},{10,... | collective-permute-start | bytes 12296 | tf_op jit(solution)/shard_map/ppermute | solution.py:202
  17.6 6.3 %collective-permute-start.2 = (bf16[2,16,128]{2,1,0:T(8,128)(2,1)S(1)}, bf16[2,16,128]{2,1,0:T(8,128)(2,1)S(1)}, u32[]{:S(2)}, u32[]{:S(2)}) collective-permute-start(bf16[2,16,128]{2,1,0:T(8,128)(2,1)S(1)} %get-tuple-element.22), channel_id=1, source_target_pairs={{0,1},{1,0},{2,3},{3,2},{4,5},{5,4},{6,7},{7,6},{8,9},{9,8},{10,11... | collective-permute-start | bytes 24584 | tf_op jit(solution)/shard_map/ppermute | solution.py:202
  17.6 6.3 %collective-permute-start.3 = (bf16[2,16,128]{2,1,0:T(8,128)(2,1)S(1)}, bf16[2,16,128]{2,1,0:T(8,128)(2,1)S(1)}, u32[]{:S(2)}, u32[]{:S(2)}) collective-permute-start(bf16[2,16,128]{2,1,0:T(8,128)(2,1)S(1)} %get-tuple-element.23), channel_id=1, source_target_pairs={{0,7},{1,2},{2,1},{3,4},{4,3},{5,6},{6,5},{7,0},{8,15},{9,10},{10,... | collective-permute-start | bytes 24584 | tf_op jit(solution)/shard_map/ppermute | solution.py:202

commit v9 on v5

--- a/solution.py
+++ b/solution.py
@@ -283,7 +283,7 @@
             pltpu.VMEM((steps, far_len // steps, far_cores.shape[1]), BF),
             pltpu.VMEM(near_out.shape, BF),
             pltpu.VMEM((far_len, chunks * lanes), BF),
-            pltpu.VMEM((2 * devices * chunks, lanes), F32),
+            pltpu.VMEM((2 * devices * chunks + 8, lanes), F32),
             pltpu.VMEM((devices, 2 * chunks, lanes), BF),
             pltpu.VMEM(currents.shape, BF),
             pltpu.SemaphoreType.DMA((9 + steps,)),
@@ -294,7 +294,7 @@
     sec_a, sec_b = swap(sec_a, "sec", 0), swap(sec_b, "sec", 1)
     az_a, az_b = swap(az_a, "az", 0), swap(az_b, "az", 1)
 
-    parts = 2
+    parts = 1
     base, near_weights, far_weights = call(
         solve_kernel,
         (

time: 27.3 us -> 27.3 us (level)
  transfers between devices with their start and end apart: 5 -> 5, of which waited for: 1 -> 1; matrix products, arithmetic and copies ran while one was open for 0% -> 0% of each run, Pallas kernels for 19% -> 18%
where the time goes in v9:
time: 27.3 us; the launch traced here: 27.2 us
  starting transfers between devices  15.2 us (56%)
  Pallas kernels  10 us (37%)
  waiting for transfers between devices  1.9 us (7%)
    all_to_all x1, starting transfers between devices, local(): lax.all_to_all(packed, ('core', 'sec', 'y'), split_axis=0, concat_axis=0,...  11.5 us
    pallas_call x1, Pallas kernels, local(): call(solve_kernel, (shape((2, rhs_count, row_count), F32), shape((2, 3 *...  4.68 us
    pallas_call x1, Pallas kernels, local(): call(send_kernel, (shape((devices, 2 * chunks, lanes)), piece, piece, pai...  3.95 us
    ppermute x4, starting transfers between devices, swap(): return lax.ppermute(value, ALL, route)  3.69 us
    all_to_all x1, waiting for transfers between devices, local(): lax.all_to_all(packed, ('core', 'sec', 'y'), split_axis=0, concat_axis=0,...  1.89 us
    pallas_call x1, Pallas kernels, local(): call(far_in_kernel, shape(right_side.shape, F32), [VMEM] * 3, 2 * 2 * rhs...  1.07 us
  transfers between devices with their start and end apart: 5, of which 1 were waited for; matrix products, arithmetic and copies ran while one was open for 0% of the time, Pallas kernels for 18%

profile of v9, /device:TPU:1, one launch (start us, length us, event | category | flops | bytes accessed | tf_op | source)
XLA Modules:
  0.0 27.2 jit_solution(13432186043725589503)
XLA Ops:
  0.0 3.9 %shard_map.118 = (bf16[128,8,128]{2,1,0:T(8,128)(2,1)}, bf16[16,128]{1,0:T(8,128)(2,1)S(1)}, bf16[16,128]{1,0:T(8,128)(2,1)S(1)}, bf16[2,16,128]{2,1,0:T(8,128)(...) custom-call(s32[2]{0:T(128)} %counts_hbm.1, ...), custom_call_target="tpu_custom_call" | custom-call | flops 805306368 | bytes 3145728 | tf_op jit(solution)/shard_map/pallas_call | solution.py:261
  4.0 11.5 %all-to-all-start = ((bf16[128,8,128]{2,1,0:T(8,128)(2,1)}), bf16[128,8,128]{2,1,0:T(8,128)(2,1)S(1)}, u32[]{:S(2)}, u32[]{:S(2)}) async-start(bf16[128,8,128]{2,1,0:T(8,128)(2,1)} %get-tuple-element.15), calls=%async_computation | async-start | bytes 524288 | tf_op jit(solution)/shard_map/all_to_all | solution.py:293
  15.5 1.5 %collective-permute-start = (bf16[16,128]{1,0:T(8,128)(2,1)S(1)}, bf16[16,128]{1,0:T(8,128)(2,1)S(1)}, u32[]{:S(2)}, u32[]{:S(2)}) collective-permute-start(bf16[16,128]{1,0:T(8,128)(2,1)S(1)} %get-tuple-element.17), channel_id=1, source_target_pairs={{0,8},{1,9},{2,10},{3,11},{4,12},{5,13},{6,14},{7,15},{8,0},{9,1},... | collective-permute-start | bytes 12296 | tf_op jit(solution)/shard_map/ppermute | solution.py:209
  16.9 0.6 %collective-permute-start.1 = (bf16[16,128]{1,0:T(8,128)(2,1)S(1)}, bf16[16,128]{1,0:T(8,128)(2,1)S(1)}, u32[]{:S(2)}, u32[]{:S(2)}) collective-permute-start(bf16[16,128]{1,0:T(8,128)(2,1)S(1)} %get-tuple-element.18), channel_id=1, source_target_pairs={{0,1},{1,0},{2,3},{3,2},{4,5},{5,4},{6,7},{7,6},{8,16},{9,17},{10,... | collective-permute-start | bytes 12296 | tf_op jit(solution)/shard_map/ppermute | solution.py:209
  17.6 0.0 collective-permute-start.2
  17.6 1.6 %collective-permute-start.3 = (bf16[2,16,128]{2,1,0:T(8,128)(2,1)S(1)}, bf16[2,16,128]{2,1,0:T(8,128)(2,1)S(1)}, u32[]{:S(2)}, u32[]{:S(2)}) collective-permute-start(bf16[2,16,128]{2,1,0:T(8,128)(2,1)S(1)} %get-tuple-element.20), channel_id=1, source_target_pairs={{0,7},{1,2},{2,1},{3,4},{4,3},{5,6},{6,5},{7,0},{8,15},{9,10},{10,... | collective-permute-start | bytes 24584 | tf_op jit(solution)/shard_map/ppermute | solution.py:209
  19.2 4.7 %shard_map.119 = (f32[2,16,1024]{2,1,0:T(8,128)S(1)}, bf16[2,384,1024]{2,1,0:T(8,128)(2,1)S(1)}, bf16[64,1024]{1,0:T(8,128)(2,1)S(1)}) custom-call(f32[2,1,1024]{2,1,0:T(1,128)S(1)} %get-tuple-element.16.keep, bf16[2,16,128]{2,1,0:T(8,128)(2,1)S(1)} %get-tuple-element.21.kept, f32[2,16,1024]{2,1,0:T(8,128)} %right_hbm.1, bf16[2,32,1024]{2,1,0:T(8,128)(2,1)} %basis_hbm.3, ...), custom_call_target="tpu_custom_call" | custom-call | flops 1879048192 | bytes 4194304 | tf_op jit(solution)/shard_map/pallas_call | solution.py:298
  23.8 0.0 collective-permute-done.sec_a
  23.9 0.0 collective-permute-done.1.sec_b
  23.9 0.0 collective-permute-done.2.az_a
  23.9 0.0 collective-permute-done.3.az_b
  23.9 0.3 %shard_map.120.solved = f32[2,16,1024]{2,1,0:T(8,128)S(1)} custom-call(f32[2,1,1024]{2,1,0:T(1,128)S(1)} %get-tuple-element.16.keep, bf16[16,128]{1,0:T(8,128)(2,1)S(1)} %collective-permute-done.sec_a, bf16[16,128]{1,0:T(8,128)(2,1)S(1)} %collective-permute-done.1.sec_b, bf16[2,16,128]{2,1,0:T(8,128)(2,1)S(1)} %collective-permute-done.2.az_a, ...), custom_call_target="tpu_custom_call" | custom-call | flops 25165824 | bytes 2097152 | tf_op jit(solution)/shard_map/pallas_call | solution.py:318
  24.2 1.9 %all-to-all-done.received = bf16[128,8,128]{2,1,0:T(8,128)(2,1)S(1)} async-done(((bf16[128,8,128]{2,1,0:T(8,128)(2,1)}), bf16[128,8,128]{2,1,0:T(8,128)(2,1)S(1)}, u32[]{:S(2)}, u32[]{:S(2)}) %all-to-all-start) | async-done | bytes 262176 | tf_op jit(solution)/shard_map/all_to_all | solution.py:293
  26.1 1.1 %shard_map.121 = f32[2,16,1024]{2,1,0:T(8,128)} custom-call(bf16[128,8,128]{2,1,0:T(8,128)(2,1)S(1)} %all-to-all-done.received, f32[2,16,1024]{2,1,0:T(8,128)S(1)} %shard_map.120.solved, bf16[64,1024]{1,0:T(8,128)(2,1)S(1)} %get-tuple-element.24.far_weights), custom_call_target="tpu_custom_call" | custom-call | flops 2097152 | bytes 262144 | tf_op jit(solution)/shard_map/pallas_call | solution.py:327
Async XLA Ops:
  4.0 22.1 %all-to-all-start = ((bf16[128,8,128]{2,1,0:T(8,128)(2,1)}), bf16[128,8,128]{2,1,0:T(8,128)(2,1)S(1)}, u32[]{:S(2)}, u32[]{:S(2)}) async-start(bf16[128,8,128]{2,1,0:T(8,128)(2,1)} %get-tuple-element.15), calls=%async_computation | async-start | bytes 524288 | tf_op jit(solution)/shard_map/all_to_all | solution.py:293
  15.5 8.4 %collective-permute-start = (bf16[16,128]{1,0:T(8,128)(2,1)S(1)}, bf16[16,128]{1,0:T(8,128)(2,1)S(1)}, u32[]{:S(2)}, u32[]{:S(2)}) collective-permute-start(bf16[16,128]{1,0:T(8,128)(2,1)S(1)} %get-tuple-element.17), channel_id=1, source_target_pairs={{0,8},{1,9},{2,10},{3,11},{4,12},{5,13},{6,14},{7,15},{8,0},{9,1},... | collective-permute-start | bytes 12296 | tf_op jit(solution)/shard_map/ppermute | solution.py:209
  16.9 6.9 %collective-permute-start.1 = (bf16[16,128]{1,0:T(8,128)(2,1)S(1)}, bf16[16,128]{1,0:T(8,128)(2,1)S(1)}, u32[]{:S(2)}, u32[]{:S(2)}) collective-permute-start(bf16[16,128]{1,0:T(8,128)(2,1)S(1)} %get-tuple-element.18), channel_id=1, source_target_pairs={{0,1},{1,0},{2,3},{3,2},{4,5},{5,4},{6,7},{7,6},{8,16},{9,17},{10,... | collective-permute-start | bytes 12296 | tf_op jit(solution)/shard_map/ppermute | solution.py:209
  17.6 6.3 %collective-permute-start.2 = (bf16[2,16,128]{2,1,0:T(8,128)(2,1)S(1)}, bf16[2,16,128]{2,1,0:T(8,128)(2,1)S(1)}, u32[]{:S(2)}, u32[]{:S(2)}) collective-permute-start(bf16[2,16,128]{2,1,0:T(8,128)(2,1)S(1)} %get-tuple-element.19), channel_id=1, source_target_pairs={{0,1},{1,0},{2,3},{3,2},{4,5},{5,4},{6,7},{7,6},{8,9},{9,8},{10,11... | collective-permute-start | bytes 24584 | tf_op jit(solution)/shard_map/ppermute | solution.py:209
  17.6 6.3 %collective-permute-start.3 = (bf16[2,16,128]{2,1,0:T(8,128)(2,1)S(1)}, bf16[2,16,128]{2,1,0:T(8,128)(2,1)S(1)}, u32[]{:S(2)}, u32[]{:S(2)}) collective-permute-start(bf16[2,16,128]{2,1,0:T(8,128)(2,1)S(1)} %get-tuple-element.20), channel_id=1, source_target_pairs={{0,7},{1,2},{2,1},{3,4},{4,3},{5,6},{6,5},{7,0},{8,15},{9,10},{10,... | collective-permute-start | bytes 24584 | tf_op jit(solution)/shard_map/ppermute | solution.py:209
